TPU v7x, 32 devices: a whole 2x2x4 slice. The times are simulated.
32 devices in a mesh: wide: 16 (over z, y, x), narrow: 2 (over core).
Axes of the slice: x: 2, y: 2, z: 4, core: 2. Of those that a mesh axis runs over, the one named last changes fastest.
Arguments:
- voltages: bfloat16 [512, 1048576], P('wide', 'narrow'), may hold values from -6 to 6
- following: bfloat16 [512, 30720], P('wide'), may hold values from -6 to 6
Outputs:
- visibilities: float32 [1024, 2, 512, 512], P(('wide', 'narrow'))
All inputs are finite; a program needn't handle non-finite values.
Results may differ from a plain program's by a relative error of at most 0.0028.
Values may be sent and summed in bfloat16 or wider, within the bound.
No kernel may reach another device: no remote copies, remote signals or barrier semaphores. Data moves between devices by JAX's collectives and lax.ppermute only.
A program may use at most 384 MiB of HBM per device.

v0:
```python
import math

import jax
import jax.numpy as jnp
from jax import lax
from jax.sharding import PartitionSpec as P

FFT_LEN = 2048
CHANNELS = 1024
TAPS = 16


def from_behind(x, axis, by):
    size = lax.axis_size(axis)
    pairs = [(i, i + by) for i in range(size) if 0 <= i + by < size]
    return lax.ppermute(x, axis, pairs)


def pfb_window(block_len, tap_count):
    length_all = tap_count * block_len
    sample_pos = jnp.arange(length_all, dtype=jnp.float32)
    centred = (sample_pos + 0.5 - length_all / 2.0) / block_len
    taper = 0.5 - 0.5 * jnp.cos(2.0 * jnp.pi * (sample_pos + 0.5) / length_all)
    return jnp.sinc(centred) * taper


def phase_table(first_len, second_len, modulus):
    first_idx = jnp.arange(first_len, dtype=jnp.int32)[:, None]
    second_idx = jnp.arange(second_len, dtype=jnp.int32)[None, :]
    turns = (first_idx * second_idx % modulus).astype(jnp.float32)
    angles = 2.0 * jnp.pi * turns / modulus
    return (jnp.cos(angles), jnp.sin(angles))


def shards(voltages, following):
    local_inputs, local_span = voltages.shape
    local_spec = local_span // FFT_LEN
    halo_len = (TAPS - 1) * FFT_LEN
    leading = voltages[:, :halo_len]
    shifted = from_behind(leading, "narrow", -1)
    is_final = lax.axis_index("narrow") == lax.axis_size("narrow") - 1
    after_rows = jnp.where(is_final, following, shifted)
    samples = jnp.concatenate([voltages, after_rows], axis=1)
    samples = samples.reshape(local_inputs, local_spec + TAPS - 1, FFT_LEN)
    blocks = jnp.transpose(samples, (2, 0, 1))
    weights_taps = pfb_window(FFT_LEN, TAPS).reshape(TAPS, FFT_LEN)
    filtered = jnp.zeros((FFT_LEN, local_inputs, local_spec), jnp.float32)
    for tap_index in range(TAPS):
        filtered = filtered + weights_taps[tap_index][:, None, None] * blocks[
            :, :, tap_index : tap_index + local_spec
        ].astype(jnp.float32)
    bit_count = FFT_LEN.bit_length() - 1
    outer_len = 2 ** (bit_count // 2)
    inner_len = FFT_LEN // outer_len
    kept_len = inner_len // 2
    row_count = local_inputs * local_spec
    folded = filtered.reshape(outer_len, inner_len, row_count)
    highest = lax.Precision.HIGHEST
    cos_outer, sin_outer = phase_table(outer_len, outer_len, outer_len)
    first_real = jnp.einsum("abr,ac->cbr", folded, cos_outer, precision=highest)
    first_imag = -jnp.einsum("abr,ac->cbr", folded, sin_outer, precision=highest)
    cos_twiddle, sin_twiddle = phase_table(outer_len, inner_len, FFT_LEN)
    cos_twiddle = cos_twiddle[:, :, None]
    sin_twiddle = sin_twiddle[:, :, None]
    turned_real = first_real * cos_twiddle + first_imag * sin_twiddle
    turned_imag = first_imag * cos_twiddle - first_real * sin_twiddle
    cos_inner, sin_inner = phase_table(inner_len, kept_len, inner_len)
    final_real = jnp.einsum("cbr,bd->dcr", turned_real, cos_inner, precision=highest) + jnp.einsum(
        "cbr,bd->dcr", turned_imag, sin_inner, precision=highest
    )
    final_imag = jnp.einsum("cbr,bd->dcr", turned_imag, cos_inner, precision=highest) - jnp.einsum(
        "cbr,bd->dcr", turned_real, sin_inner, precision=highest
    )
    scaling = 1.0 / math.sqrt(FFT_LEN)
    final_real = final_real.reshape(CHANNELS, local_inputs, local_spec) * scaling
    final_imag = final_imag.reshape(CHANNELS, local_inputs, local_spec) * scaling
    spectra = jnp.stack([final_real, final_imag], axis=1).astype(jnp.bfloat16)
    gathered = lax.all_to_all(
        lax.all_to_all(spectra, "wide", split_axis=0, concat_axis=2, tiled=True),
        "narrow",
        split_axis=0,
        concat_axis=3,
        tiled=True,
    )
    chan_dev = gathered.shape[0]
    all_inputs = gathered.shape[2]
    time_len = gathered.shape[3]
    stacked = gathered.reshape(chan_dev, 2 * all_inputs, time_len)
    gram = lax.dot_general(
        stacked, stacked, (((2,), (2,)), ((0,), (0,))), preferred_element_type=jnp.float32
    )
    vis_real = gram[:, :all_inputs, :all_inputs] + gram[:, all_inputs:, all_inputs:]
    vis_imag = gram[:, all_inputs:, :all_inputs] - gram[:, :all_inputs, all_inputs:]
    return jnp.stack([vis_real, vis_imag], axis=1) / time_len


def solution(mesh):
    in_specs = (P("wide", "narrow"), P("wide", None))
    out_specs = P(("wide", "narrow"), None, None, None)
    return jax.shard_map(shards, mesh=mesh, in_specs=in_specs, out_specs=out_specs, check_vma=False)
```

profile of v0, /device:TPU:0, one launch (start us, length us, event | category | flops | bytes accessed | tf_op | source)
XLA Modules:
  0.0 2310.1 jit_solution(7618350981123420380)
XLA Ops:
  0.0 1.7 slice.128
  1.7 1.3 collective-permute-start
  3.0 0.8 fusion.64
  3.8 0.6 fusion.18
  4.4 3.3 collective-permute-done
  7.7 1.8 broadcast_select_fusion
  9.4 24.0 %pad_maximum_fusion = bf16[32,555008]{1,0:T(8,128)(2,1)} fusion(bf16[32,30720]{1,0:T(8,128)(2,1)S(1)} %broadcast_select_fusion, bf16[32,524288]{1,0:T(8,128)(2,1)} %param.2), kind=kLoop, calls=%fused_computation.12 | loop fusion | flops 71041024 | bytes 71041024 | tf_op jit(solution)/shard_map/concatenate | solution.py:43
  33.4 45.0 %reshape.123 = bf16[32,271,2048]{2,1,0:T(8,128)(2,1)} reshape(bf16[32,555008]{1,0:T(8,128)(2,1)} %pad_maximum_fusion) | data formatting | bytes 71041024 | tf_op jit(solution)/shard_map/reshape | solution.py:44
  78.4 244.7 %multiply_add_fusion.1 = f32[2048,32,256]{0,2,1:T(8,128)} fusion(bf16[2048,32,271]{0,2,1:T(8,128)(2,1)} %bitcast.60, f32[2048]{0:T(1024)S(1)} %get-tuple-element.10, f32[2048]{0:T(1024)S(1)} %get-tuple-element.11, f32[2048]{0:T(1024)S(1)} %get-tuple-element.12, f32[2048]{0:T(1024)S(1)} %get-tuple-element.13, f32[2048]{0:T(1024)S(1)} %get-tuple-element.14, ...), kind=kLoop, calls=%fused_computation.3 | loop fusion | flops 788529152 | bytes 604110848 | tf_op jit(solution)/shard_map/add | solution.py:49
  323.1 107.5 %reshape.130 = f32[32,64,8192]{1,0,2:T(8,128)} reshape(f32[2048,32,256]{0,2,1:T(8,128)} %multiply_add_fusion.1) | data formatting | bytes 134217728 | tf_op jit(solution)/shard_map/reshape | solution.py:57
  430.5 100.2 %copy.33 = f32[32,64,8192]{2,0,1:T(8,128)} copy(f32[32,64,8192]{1,0,2:T(8,128)} %reshape.130) | data formatting | bytes 134217728 | tf_op jit(solution)/shard_map/reshape | solution.py:57
  530.7 0.0 copy-start
  530.7 0.0 copy-start.1
  530.7 66.5 %fusion.57 = f32[32,64,8192]{2,0,1:T(8,128)} fusion(f32[32,64,8192]{2,0,1:T(8,128)} %copy.33), kind=kOutput, calls=%fused_computation.81 | convolution fusion | flops 6442465280 | bytes 134217728 | tf_op jit(solution)/shard_map/abr,ac->cbr/dot_general | solution.py:61
  597.2 0.0 copy-done
  597.2 0.0 copy-done.1
  597.2 104.0 %multiply_add_fusion = (f32[32,64,8192]{2,0,1:T(8,128)}, f32[32,64,8192]{2,0,1:T(8,128)}) fusion(f32[32,64,8192]{2,0,1:T(8,128)} %fusion.57, f32[32,64]{0,1:T(8,128)S(1)} %copy-done, f32[32,64]{0,1:T(8,128)S(1)} %copy-done.1, f32[32,64,8192]{2,0,1:T(8,128)} %copy.33), kind=kOutput, calls=%fused_computation.2 | convolution fusion | flops 6559905792 | bytes 268451840 | tf_op jit(solution)/shard_map/abr,ac->cbr/dot_general | solution.py:60
  701.2 86.7 %fusion = f32[32,32,8192]{2,0,1:T(8,128)} fusion(f32[32,64,8192]{2,0,1:T(8,128)} %get-tuple-element.6), kind=kOutput, calls=%fused_computation.4 | convolution fusion | flops 6442479616 | bytes 100663296 | tf_op jit(solution)/shard_map/cbr,bd->dcr/dot_general | solution.py:71
  787.9 85.8 %fusion.2 = f32[32,32,8192]{2,0,1:T(8,128)} fusion(f32[32,64,8192]{2,0,1:T(8,128)} %get-tuple-element.6), kind=kOutput, calls=%fused_computation.6 | convolution fusion | flops 6442479616 | bytes 100663296 | tf_op jit(solution)/shard_map/cbr,bd->dcr/dot_general | solution.py:68
  873.7 92.7 %multiply_convert_fusion.1 = bf16[32,32,8192]{2,0,1:T(8,128)(2,1)} fusion(f32[32,32,8192]{2,0,1:T(8,128)} %fusion.2, f32[32,64,8192]{2,0,1:T(8,128)} %get-tuple-element.5), kind=kOutput, calls=%fused_computation.19 | convolution fusion | flops 6467645440 | bytes 117440512 | tf_op jit(solution)/shard_map/cbr,bd->dcr/dot_general | solution.py:68
  966.5 90.6 %multiply_convert_fusion = bf16[32,32,8192]{2,0,1:T(8,128)(2,1)} fusion(f32[32,32,8192]{2,0,1:T(8,128)} %fusion, f32[32,64,8192]{2,0,1:T(8,128)} %get-tuple-element.5), kind=kOutput, calls=%fused_computation.18 | convolution fusion | flops 6467645440 | bytes 117440512 | tf_op jit(solution)/shard_map/cbr,bd->dcr/dot_general | solution.py:71
  1057.1 0.0 slice-start
  1057.1 0.0 slice-start.1
  1057.1 15.1 copy.40
  1072.2 0.0 slice-start.2
  1072.2 0.0 slice-start.3
  1072.2 8.6 copy.48
  1080.8 0.0 slice-done
  1080.8 0.0 slice-done.1
  1080.8 0.0 slice-done.2
  1080.8 0.0 slice-done.3
  1080.9 21.2 copy.37
  1102.1 8.3 copy.47
  1110.4 23.0 pad_maximum_fusion.1
  1133.3 23.3 %copy.41 = bf16[1024,2,32,256]{3,2,1,0:T(8,128)(2,1)} copy(bf16[1024,2,32,256]{3,2,0,1:T(8,128)(2,1)} %pad_maximum_fusion.1) | data formatting | bytes 67108864 | tf_op jit(solution)/shard_map/stack | solution.py:77
  1156.6 732.9 %all_to_all.33 = bf16[1024,2,32,256]{3,2,1,0:T(8,128)(2,1)} all-to-all(bf16[1024,2,32,256]{3,2,1,0:T(8,128)(2,1)} %copy.41), channel_id=1, replica_groups=mesh['wide'=16,'narrow'=2] {'wide'}, dimensions={0} | all-to-all | bytes 67108864 | tf_op jit(solution)/shard_map/all_to_all | solution.py:79
  1889.5 23.1 copy.42
  1912.6 57.8 %all_to_all.34 = bf16[64,2,512,256]{3,2,1,0:T(8,128)(2,1)} all-to-all(bf16[64,2,512,256]{3,2,1,0:T(8,128)(2,1)} %bitcast.62), channel_id=1, replica_groups=mesh['wide'=16,'narrow'=2] {'narrow'}, dimensions={0} | all-to-all | bytes 67108864 | tf_op jit(solution)/shard_map/all_to_all | solution.py:78
  1970.4 60.3 %copy.43 = bf16[32,2,512,2,256]{4,3,2,1,0:T(2,128)(2,1)} copy(bf16[32,2,512,2,256]{4,2,1,0,3:T(8,128)(2,1)} %bitcast.63) | data formatting | bytes 67108864 | tf_op jit(solution)/shard_map/all_to_all | solution.py:78
  2030.7 52.7 %reshape.125 = bf16[32,1024,512]{2,1,0:T(8,128)(2,1)} reshape(bf16[32,2,512,2,256]{4,3,2,1,0:T(2,128)(2,1)} %copy.43) | data formatting | bytes 67108864 | tf_op jit(solution)/shard_map/reshape | solution.py:88
  2083.4 71.9 %fusion.106 = f32[32,1024,1024]{2,1,0:T(8,128)} fusion(bf16[32,1024,512]{2,1,0:T(8,128)(2,1)} %reshape.125), kind=kOutput, calls=%fused_computation.124 | convolution fusion | flops 34359738368 | bytes 167772160 | tf_op jit(solution)/shard_map/dot_general | solution.py:89
  2155.3 65.6 %fusion.9 = (f32[32,1,512,512]{3,2,0,1:T(8,128)}, f32[32,1,512,512]{3,2,0,1:T(8,128)}) fusion(f32[32,1024,1024]{2,1,0:T(8,128)} %fusion.106), kind=kLoop, calls=%fused_computation.16 | loop fusion | flops 16777216 | bytes 201326592 | tf_op jit(solution)/shard_map/stack | solution.py:94
  2220.9 44.9 %maximum_multiply_fusion = f32[32,2,512,512]{3,2,0,1:T(8,128)} fusion(f32[32,1,512,512]{3,2,0,1:T(8,128)} %get-tuple-element.8, f32[32,1,512,512]{3,2,0,1:T(8,128)} %get-tuple-element.7), kind=kLoop, calls=%fused_computation | loop fusion | flops 33554432 | bytes 134217728 | tf_op jit(solution)/shard_map/div | solution.py:94
  2265.8 44.0 %copy.44 = f32[32,2,512,512]{3,2,1,0:T(8,128)} copy(f32[32,2,512,512]{3,2,0,1:T(8,128)} %maximum_multiply_fusion) | data formatting | bytes 134217728 | tf_op jit(solution)/shard_map/div | solution.py:94
  (2 shorter events, 0.0 us)
Async XLA Ops:
  1.7 6.0 collective-permute-start
  530.7 66.5 %copy-start = (f32[32,64]{0,1:T(8,128)S(1)}, f32[32,64]{0,1:T(8,128)}, u32[]{:S(2)}) copy-start(f32[32,64]{0,1:T(8,128)} %get-tuple-element.25) | copy-start | bytes 24580
  530.7 66.5 %copy-start.1 = (f32[32,64]{0,1:T(8,128)S(1)}, f32[32,64]{0,1:T(8,128)}, u32[]{:S(2)}) copy-start(f32[32,64]{0,1:T(8,128)} %get-tuple-element.26) | copy-start | bytes 24580
  1057.1 23.8 %slice-start = ((s8[16777216]{0:T(1024)(128)(4,1)}), s8[4194304]{0:T(1024)(128)(4,1)S(1)}, s32[]{:S(2)}) async-start(s8[16777216]{0:T(1024)(128)(4,1)} %bitcast.64), calls=%async_computation.2 | async-start | bytes 8388608
  1057.1 23.8 %slice-start.1 = ((s8[16777216]{0:T(1024)(128)(4,1)}), s8[4194304]{0:T(1024)(128)(4,1)S(1)}, s32[]{:S(2)}) async-start(s8[16777216]{0:T(1024)(128)(4,1)} %bitcast.64), calls=%async_computation.3 | async-start | bytes 8388608
  1072.2 8.6 slice-start.2
  1072.2 8.6 slice-start.3
where the time goes:
time: 2320 us; the launch traced here: 2310 us
  blocking collectives  791 us (34%)
  matrix products  598 us (26%)
  local copies, waits for them, and re-layouts  511 us (22%)
  other arithmetic  405 us (17%)
    all_to_all x1, blocking collectives, shards(): lax.all_to_all(spectra, 'wide', split_axis=0, concat_axis=2, tiled=True)  733 us
    add x1, other arithmetic, shards(): filtered + weights_taps[tap_index][:, None, None] * blocks[:, :, tap_inde...  245 us
    reshape x2, local copies, waits for them, and re-layouts, shards(): folded = filtered.reshape(outer_len, inner_len, row_count)  208 us
    dot_general x1, matrix products, shards(): first_real = jnp.einsum('abr,ac->cbr', folded, cos_outer, precision=highest)  104 us
    dot_general x1, matrix products, shards(): jnp.einsum('cbr,bd->dcr', turned_real, cos_inner, precision=highest)  92.7 us
    dot_general x1, matrix products, shards(): jnp.einsum('cbr,bd->dcr', turned_real, sin_inner, precision=highest)  90.6 us
    dot_general x1, matrix products, shards(): jnp.einsum('cbr,bd->dcr', turned_imag, cos_inner, precision=highest)  86.7 us
    dot_general x1, matrix products, shards(): jnp.einsum('cbr,bd->dcr', turned_imag, sin_inner, precision=highest)  85.8 us
  transfers between devices with their start and end apart: 1, of which 1 were waited for; matrix products, arithmetic and copies ran while one was open for 0% of the time, Pallas kernels for 0%

commit v1 on v0

v1 whole, which is shorter than its diff:
```python
import functools
import math

import jax
import jax.numpy as jnp
import ml_dtypes
import numpy as np
from jax import lax
from jax.experimental import pallas as pl
from jax.experimental.pallas import tpu as pltpu
from jax.sharding import PartitionSpec as P

FFT_LEN = 2048
CHANNELS = 1024
TAPS = 16
FOLD = FFT_LEN // 2
SPAN = 128
GROUPS = 4
BATCH = 8
COLS = 256
VMEM = 56 * 1024 * 1024
AXES = ("wide", "narrow")


def pfb_window():
    n = np.arange(TAPS * FFT_LEN, dtype=np.float64)
    total = TAPS * FFT_LEN
    taper = 0.5 - 0.5 * np.cos(2.0 * np.pi * (n + 0.5) / total)
    window = np.sinc((n + 0.5 - total / 2) / FFT_LEN) * taper
    return window.astype(np.float32).reshape(TAPS, FFT_LEN)


def split16(values):
    high = values.astype(ml_dtypes.bfloat16)
    low = (values - high.astype(np.float64)).astype(ml_dtypes.bfloat16)
    return high, low


def dft_tables(n_dev):
    chan_dev = CHANNELS // n_dev
    cg = chan_dev // GROUPS
    g, p, d, h = np.meshgrid(
        np.arange(GROUPS), np.arange(2), np.arange(n_dev), np.arange(cg // 2), indexing="ij"
    )
    chan = d * chan_dev + g * cg + 2 * h + p
    turns = chan[..., None] * np.arange(FOLD) % FFT_LEN
    angles = 2.0 * np.pi * turns / FFT_LEN
    table = np.stack([np.cos(angles), -np.sin(angles)], axis=-2) / math.sqrt(FFT_LEN)
    return split16(table.reshape(GROUPS, 2, CHANNELS // GROUPS, FOLD))


def filter_kernel(x_ref, halo_ref, w_ref, *rest):
    f_ref, even_ref, odd_ref = rest[-3:]
    n_in = x_ref.shape[0]
    column0 = pl.program_id(0) * COLS

    def load(ref, t, k):
        tile = ref[:, pl.ds(pl.multiple_of(t * FFT_LEN + k, 128), 128)].astype(jnp.float32)
        return tile.reshape(n_in // 8, 8, 128)

    def fir(tiles, k):
        weights = [w_ref[p, :, pl.ds(pl.multiple_of(k, 128), 128)][None] for p in range(TAPS)]
        outs = []
        for j in range(BATCH):
            total = weights[0] * tiles[j]
            for p in range(1, TAPS):
                total = total + weights[p] * tiles[j + p]
            outs.append(total)
        return outs

    def emit(m0, first, second):
        for j in range(BATCH):
            rows = pl.ds(m0 + j, n_in, stride=SPAN)
            even_ref[rows, :] = (first[j] + second[j]).reshape(n_in, 128)
            odd_ref[rows, :] = (first[j] - second[j]).reshape(n_in, 128)

    inner = (SPAN - TAPS + 1) // BATCH
    for kt in range(COLS // 128):
        k = column0 + kt * 128

        def body(step, _, k=k):
            m0 = step * BATCH
            both = []
            for kk in (k, k + FOLD):
                both.append(fir([load(x_ref, m0 + t, kk) for t in range(BATCH + TAPS - 1)], kk))
            emit(m0, *both)
            return 0

        lax.fori_loop(0, inner, body, 0)
        for step in range(inner, SPAN // BATCH):
            m0 = step * BATCH
            both = []
            for kk in (k, k + FOLD):
                tiles = []
                for t in range(m0, m0 + BATCH + TAPS - 1):
                    tiles.append(load(x_ref, t, kk) if t < SPAN else load(halo_ref, t - SPAN, kk))
                both.append(fir(tiles, kk))
            emit(m0, *both)

        def split(step, _, kt=kt):
            rows = pl.ds(pl.multiple_of(step * 256, 256), 256)
            for p, ref in ((0, even_ref), (1, odd_ref)):
                value = ref[rows, :]
                high = value.astype(jnp.bfloat16)
                low = (value - high.astype(jnp.float32)).astype(jnp.bfloat16)
                f_ref[p, 0, rows, pl.ds(kt * 128, 128)] = high
                f_ref[p, 1, rows, pl.ds(kt * 128, 128)] = low
            return 0

        lax.fori_loop(0, n_in * SPAN // 256, split, 0)


def filter_unit(voltages, after, weights, n_in, ig, half, halves, deps):
    width = SPAN * FFT_LEN
    if half == halves - 1:
        halo = after
        halo_spec = pl.BlockSpec((n_in, after.shape[1]), lambda i: (ig, 0))
    else:
        halo = voltages
        halo_spec = pl.BlockSpec((n_in, TAPS * FFT_LEN), lambda i: (ig, (half + 1) * SPAN // TAPS))
    rows = n_in * SPAN
    return pl.pallas_call(
        filter_kernel,
        grid=(FOLD // COLS,),
        in_specs=[
            pl.BlockSpec((n_in, width), lambda i: (ig, half)),
            halo_spec,
            pl.BlockSpec((TAPS, 8, FFT_LEN), lambda i: (0, 0, 0)),
        ]
        + [pl.BlockSpec(memory_space=pl.ANY)] * len(deps),
        out_specs=pl.BlockSpec((2, 2, rows, COLS), lambda i: (0, 0, 0, i)),
        out_shape=jax.ShapeDtypeStruct((2, 2, rows, FOLD), jnp.bfloat16),
        scratch_shapes=[pltpu.VMEM((rows, 128), jnp.float32)] * 2,
        compiler_params=pltpu.CompilerParams(vmem_limit_bytes=VMEM),
        cost_estimate=pl.CostEstimate(
            flops=rows * FFT_LEN * TAPS * 2, bytes_accessed=rows * FFT_LEN * 6, transcendentals=0
        ),
        name="filter",
    )(voltages, halo, weights, *deps)


def dft_kernel(f_ref, high_ref, low_ref, *rest):
    out_ref, held_ref = rest[-2:]
    step = pl.program_id(2)
    n_in = out_ref.shape[-2]
    n_rows = high_ref.shape[2]
    n_here = f_ref.shape[2] // SPAN
    dims = (((1,), (1,)), ((), ()))
    for pair in range(0, n_here, 2):
        take = min(2, n_here - pair)
        rows = pl.ds(pair * SPAN, take * SPAN)
        f_high = f_ref[0, 0, rows, :]
        f_low = f_ref[0, 1, rows, :]
        total = lax.dot_general(high_ref[0, 0], f_high, dims, preferred_element_type=jnp.float32)
        total += lax.dot_general(high_ref[0, 0], f_low, dims, preferred_element_type=jnp.float32)
        total += lax.dot_general(low_ref[0, 0], f_high, dims, preferred_element_type=jnp.float32)
        for j in range(take):
            at = step * n_here + pair + j
            held_ref[pl.ds(at, n_rows, stride=n_in), :] = total[:, j * SPAN : (j + 1) * SPAN]

    @pl.when(step == pl.num_programs(2) - 1)
    def _():
        n_dev, _, _, n_pair, _, _, _ = out_ref.shape
        for d in range(n_dev):
            each = n_pair * 2 * n_in
            block = held_ref[pl.ds(d * each, each), :].astype(jnp.bfloat16)
            out_ref[d, 0, 0] = block.reshape(n_pair, 2, n_in, SPAN)


def dft_unit(folded, tables, n_dev, n_in, g0, n_groups, deps):
    chan_dev = CHANNELS // n_dev
    n_pair = chan_dev // GROUPS // 2
    n_rows = CHANNELS // GROUPS
    here = min(4, n_in)
    f_rows = here * SPAN
    table_spec = pl.BlockSpec((1, 1, n_rows, FOLD), lambda g, p, i: (g0 + g, p, 0, 0))
    return pl.pallas_call(
        dft_kernel,
        grid=(n_groups, 2, n_in // here),
        in_specs=[
            pl.BlockSpec((1, 2, f_rows, FOLD), lambda g, p, i: (p, 0, i, 0)),
            table_spec,
            table_spec,
        ]
        + [pl.BlockSpec(memory_space=pl.ANY)] * len(deps),
        out_specs=pl.BlockSpec(
            (n_dev, 1, 1, n_pair, 2, n_in, SPAN), lambda g, p, i: (0, g, p, 0, 0, 0, 0)
        ),
        out_shape=jax.ShapeDtypeStruct(
            (n_dev, n_groups, 2, n_pair, 2, n_in, SPAN), jnp.bfloat16
        ),
        scratch_shapes=[pltpu.VMEM((n_rows * n_in, SPAN), jnp.float32)],
        compiler_params=pltpu.CompilerParams(vmem_limit_bytes=VMEM),
        cost_estimate=pl.CostEstimate(
            flops=n_groups * 12 * n_rows * n_in * SPAN * FOLD,
            bytes_accessed=n_groups * n_in * SPAN * FOLD * 8,
            transcendentals=0,
        ),
        name="dft",
    )(folded, *tables, *deps)


def gram_kernel(n_units, halves, n_wide, n_narrow, n_in, time_len, *refs):
    units = refs[:n_units]
    out_ref, left_ref, right_ref = refs[-3:]
    local_inputs = n_in * (n_units // halves)
    for w in range(n_wide):
        for n in range(n_narrow):
            for u in range(n_units):
                ig, half = u // halves, u % halves
                row = pl.ds(w * local_inputs + ig * n_in, n_in)
                at = (n * halves + half) * SPAN
                real = units[u][w * n_narrow + n, 0, 0, 0, 0]
                imag = units[u][w * n_narrow + n, 0, 0, 0, 1]
                right_ref[row, pl.ds(at, SPAN)] = real
                right_ref[row, pl.ds(time_len + at, SPAN)] = imag
                left_ref[row, pl.ds(at, SPAN)] = imag
                left_ref[row, pl.ds(time_len + at, SPAN)] = -real
    dims = (((1,), (1,)), ((), ()))
    right = right_ref[...]
    scale = 1.0 / time_len
    out_ref[0, 0] = lax.dot_general(right, right, dims, preferred_element_type=jnp.float32) * scale
    out_ref[0, 1] = (
        lax.dot_general(left_ref[...], right, dims, preferred_element_type=jnp.float32) * scale
    )


def gram_group(units, places, previous, n_wide, n_narrow, halves, group, n_in):
    n_dev = n_wide * n_narrow
    chan_dev = CHANNELS // n_dev
    cg = chan_dev // GROUPS
    n_units = len(units)
    inputs = n_wide * n_in * (n_units // halves)
    time_len = n_narrow * halves * SPAN
    specs = [
        pl.BlockSpec(
            (n_dev, 1, 1, 1, 2, n_in, SPAN), lambda t, at=at: (0, at, t % 2, t // 2, 0, 0, 0)
        )
        for at in places
    ]
    args = list(units)
    aliases = {}
    if previous is not None:
        specs.append(pl.BlockSpec(memory_space=pl.ANY))
        args.append(previous)
        aliases = {n_units: 0}
    return pl.pallas_call(
        functools.partial(gram_kernel, n_units, halves, n_wide, n_narrow, n_in, time_len),
        grid=(cg,),
        in_specs=specs,
        out_specs=pl.BlockSpec((1, 2, inputs, inputs), lambda t: (group * cg + t, 0, 0, 0)),
        out_shape=jax.ShapeDtypeStruct((chan_dev, 2, inputs, inputs), jnp.float32),
        scratch_shapes=[pltpu.VMEM((inputs, 2 * time_len), jnp.bfloat16)] * 2,
        input_output_aliases=aliases,
        compiler_params=pltpu.CompilerParams(vmem_limit_bytes=VMEM),
        cost_estimate=pl.CostEstimate(
            flops=cg * 8 * inputs * inputs * time_len,
            bytes_accessed=cg * inputs * (8 * inputs + 4 * time_len),
            transcendentals=0,
        ),
        name="gram",
    )(*args)


def shards(voltages, following):
    n_wide, n_narrow = lax.axis_size("wide"), lax.axis_size("narrow")
    n_dev = n_wide * n_narrow
    local_inputs, local_span = voltages.shape
    halves = local_span // (SPAN * FFT_LEN)
    n_in = min(16, local_inputs)
    in_groups = local_inputs // n_in

    leading = voltages[:, : (TAPS - 1) * FFT_LEN]
    shifted = lax.ppermute(leading, "narrow", [(i, i - 1) for i in range(1, n_narrow)])
    is_final = lax.axis_index("narrow") == n_narrow - 1
    after = jnp.where(is_final, following, shifted)

    tables = [jnp.asarray(t) for t in dft_tables(n_dev)]
    weights = jnp.asarray(np.broadcast_to(pfb_window()[:, None, :], (TAPS, 8, FFT_LEN)))

    order = [(ig, half) for half in range(halves) for ig in range(in_groups)]
    parts = []
    for index in range(len(order)):
        count = GROUPS if index in (0, len(order) - 1) else 1
        size = GROUPS // count
        parts += [(index, first, size) for first in range(0, GROUPS, size)]

    received = []
    folded = {}
    for job, (index, first, size) in enumerate(parts):
        if index not in folded:
            ig, half = order[index]
            deps = [received[job - 3]] if job >= 3 else []
            folded[index] = filter_unit(voltages, after, weights, n_in, ig, half, halves, deps)
        deps = [received[job - 2]] if job >= 2 else []
        spectra = dft_unit(folded[index], tables, n_dev, n_in, first, size, deps)
        received.append(lax.all_to_all(spectra, AXES, split_axis=0, concat_axis=0, tiled=True))

    result = None
    for group in range(GROUPS):
        units, places = [], []
        for ig in range(in_groups):
            for half in range(halves):
                index = order.index((ig, half))
                for job, (at, first, size) in enumerate(parts):
                    if at == index and first <= group < first + size:
                        units.append(received[job])
                        places.append(group - first)
        result = gram_group(
            units, places, result, n_wide, n_narrow, halves, group, n_in
        )
    return result


def solution(mesh):
    in_specs = (P("wide", "narrow"), P("wide", None))
    out_specs = P(("wide", "narrow"), None, None, None)
    return jax.shard_map(shards, mesh=mesh, in_specs=in_specs, out_specs=out_specs, check_vma=False)
```

time: 2320 us -> 946 us (0.41)
  blocking collectives: 791 us -> 0 us
  matrix products: 598 us -> 0 us
  local copies, waits for them, and re-layouts: 511 us -> 13.1 us
  Pallas kernels: 0 us -> 462 us
  waiting for transfers between devices: 3.27 us -> 418 us
  other arithmetic: 405 us -> 3.03 us
  starting transfers between devices: 1.29 us -> 45.6 us
    all_to_all x2 -> x0, blocking collectives: 791 us -> none  [the longest x1 733 us: shards(): lax.all_to_all(spectra, 'wide', split_axis=0, concat_axis=2, tiled=True)]
    dot_general x7 -> x0, matrix products: 598 us -> none  [the longest x1 104 us: shards(): first_real = jnp.einsum('abr,ac->cbr', folded, cos_outer, precision=highest)]
    pallas_call x0 -> x18, Pallas kernels: none -> 462 us  [the longest x10 213 us: dft_unit(): pl.pallas_call(dft_kernel, grid=(n_groups, 2, n_in // here), in_specs=[pl...]
    all_to_all x0 -> x10, waiting for transfers between devices: none -> 413 us  [shards(): lax.all_to_all(spectra, AXES, split_axis=0, concat_axis=0, tiled=True)]
    reshape x4 -> x0, local copies, waits for them, and re-layouts: 305 us -> none  [the longest x2 208 us: shards(): folded = filtered.reshape(outer_len, inner_len, row_count)]
    add x1 -> x0, other arithmetic: 245 us -> none  [shards(): filtered + weights_taps[tap_index][:, None, None] * blocks[:, :, tap_inde...]
    another operation x2 -> x0, other arithmetic: 88.6 us -> none  [the longest x1 65.6 us: shards(): return jnp.stack([vis_real, vis_imag], axis=1) / time_len]
    all_to_all x2 -> x0, local copies, waits for them, and re-layouts: 83.4 us -> none  [the longest x1 60.3 us: shards(): lax.all_to_all(lax.all_to_all(spectra, 'wide', split_axis=0, concat_axis=...]
  transfers between devices with their start and end apart: 1 -> 11, of which waited for: 1 -> 10; matrix products, arithmetic and copies ran while one was open for 0% -> 1% of each run, Pallas kernels for 0% -> 41%
where the time goes in v1:
time: 946 us; the launch traced here: 942 us
  Pallas kernels  462 us (49%)
  waiting for transfers between devices  418 us (44%)
  starting transfers between devices  45.6 us (5%)
  local copies, waits for them, and re-layouts  13.1 us (1%)
    all_to_all x10, waiting for transfers between devices, shards(): lax.all_to_all(spectra, AXES, split_axis=0, concat_axis=0, tiled=True)  413 us
    pallas_call x10, Pallas kernels, dft_unit(): pl.pallas_call(dft_kernel, grid=(n_groups, 2, n_in // here), in_specs=[pl...  213 us
    pallas_call x4, Pallas kernels, filter_unit(): pl.pallas_call(filter_kernel, grid=(FOLD // COLS,), in_specs=[pl.BlockSpe...  187 us
    pallas_call x4, Pallas kernels, gram_group(): pl.pallas_call(functools.partial(gram_kernel, n_units, halves, n_wide, n_...  62.6 us
    all_to_all x10, starting transfers between devices, shards(): lax.all_to_all(spectra, AXES, split_axis=0, concat_axis=0, tiled=True)  44.1 us
  transfers between devices with their start and end apart: 11, of which 10 were waited for; matrix products, arithmetic and copies ran while one was open for 1% of the time, Pallas kernels for 41%

profile of v1, /device:TPU:0, one launch (start us, length us, event | category | flops | bytes accessed | tf_op | source)
XLA Modules:
  0.0 941.8 jit_solution(9206774236618333590)
XLA Ops:
  0.0 2.0 jit_solution_.3.w_ref
  2.0 46.8 %filter.4.f_ref = bf16[2,2,2048,1024]{3,2,1,0:T(8,128)(2,1)} custom-call(bf16[32,524288]{1,0:T(8,128)(2,1)} %x_ref.7, bf16[32,524288]{1,0:T(8,128)(2,1)} %x_ref.7, f32[16,8,2048]{2,1,0:T(8,128)} %jit_solution_.3.w_ref), custom_call_target="tpu_custom_call" | custom-call | flops 134217728 | bytes 25165824 | tf_op jit(solution)/shard_map/filter/pallas_call | solution.py:122
  48.8 14.1 %dft.12 = bf16[32,1,2,4,2,16,128]{6,5,4,3,2,1,0:T(8,128)(2,1)} custom-call(bf16[2,2,2048,1024]{3,2,1,0:T(8,128)(2,1)} %filter.4.f_ref, bf16[4,2,256,1024]{3,2,1,0:T(8,128)(2,1)} %constant.12.clone.high_ref, bf16[4,2,256,1024]{3,2,1,0:T(8,128)(2,1)} %constant.13.clone.low_ref), custom_call_target="tpu_custom_call" | custom-call | flops 6442450944 | bytes 16777216 | tf_op jit(solution)/shard_map/dft/pallas_call | solution.py:177
  62.8 7.3 all-to-all-start.2
  70.1 14.1 %dft.10 = bf16[32,1,2,4,2,16,128]{6,5,4,3,2,1,0:T(8,128)(2,1)} custom-call(bf16[2,2,2048,1024]{3,2,1,0:T(8,128)(2,1)} %filter.4.f_ref, bf16[4,2,256,1024]{3,2,1,0:T(8,128)(2,1)} %constant.12.clone.high_ref, bf16[4,2,256,1024]{3,2,1,0:T(8,128)(2,1)} %constant.13.clone.low_ref), custom_call_target="tpu_custom_call" | custom-call | flops 6442450944 | bytes 16777216 | tf_op jit(solution)/shard_map/dft/pallas_call | solution.py:177
  84.2 34.8 %all-to-all-done.2.rest_0_.refs_0_ = bf16[32,1,2,4,2,16,128]{6,5,4,3,2,1,0:T(8,128)(2,1)S(1)} async-done(((bf16[32,1,2,4,2,16,128]{6,5,4,3,2,1,0:T(8,128)(2,1)}), bf16[32,1,2,4,2,16,128]{6,5,4,3,2,1,0:T(8,128)(2,1)S(1)}, u32[]{:S(2)}, u32[]{:S(2)}) %all-to-all-start.2) | async-done | bytes 2097184 | tf_op jit(solution)/shard_map/all_to_all | solution.py:297
  119.0 0.0 copy-start.3
  119.0 1.3 copy-done.3
  120.4 4.0 all-to-all-start
  124.4 14.1 %dft.13 = bf16[32,1,2,4,2,16,128]{6,5,4,3,2,1,0:T(8,128)(2,1)} custom-call(bf16[2,2,2048,1024]{3,2,1,0:T(8,128)(2,1)} %filter.4.f_ref, bf16[4,2,256,1024]{3,2,1,0:T(8,128)(2,1)} %constant.12.clone.high_ref, bf16[4,2,256,1024]{3,2,1,0:T(8,128)(2,1)} %constant.13.clone.low_ref, bf16[32,1,2,4,2,16,128]{6,5,4,3,2,1,0:T(8,128)(2,1)} %copy-done.3), custom_call_target="tpu_custom_call" | custom-call | flops 6442450944 | bytes 16777216 | tf_op jit(solution)/shard_map/dft/pallas_call | solution.py:177
  138.5 34.8 %all-to-all-done.rest_0_.refs_0_ = bf16[32,1,2,4,2,16,128]{6,5,4,3,2,1,0:T(8,128)(2,1)S(1)} async-done(((bf16[32,1,2,4,2,16,128]{6,5,4,3,2,1,0:T(8,128)(2,1)}), bf16[32,1,2,4,2,16,128]{6,5,4,3,2,1,0:T(8,128)(2,1)S(1)}, u32[]{:S(2)}, u32[]{:S(2)}) %all-to-all-start) | async-done | bytes 2097184 | tf_op jit(solution)/shard_map/all_to_all | solution.py:297
  173.3 0.0 copy-start
  173.3 1.3 copy-done
  174.6 4.1 all-to-all-start.3
  178.7 14.1 %dft.11 = bf16[32,1,2,4,2,16,128]{6,5,4,3,2,1,0:T(8,128)(2,1)} custom-call(bf16[2,2,2048,1024]{3,2,1,0:T(8,128)(2,1)} %filter.4.f_ref, bf16[4,2,256,1024]{3,2,1,0:T(8,128)(2,1)} %constant.12.clone.high_ref, bf16[4,2,256,1024]{3,2,1,0:T(8,128)(2,1)} %constant.13.clone.low_ref, bf16[32,1,2,4,2,16,128]{6,5,4,3,2,1,0:T(8,128)(2,1)} %copy-done), custom_call_target="tpu_custom_call" | custom-call | flops 6442450944 | bytes 16777216 | tf_op jit(solution)/shard_map/dft/pallas_call | solution.py:177
  192.8 34.8 %all-to-all-done.3.rest_0_.refs_0_ = bf16[32,1,2,4,2,16,128]{6,5,4,3,2,1,0:T(8,128)(2,1)} async-done(((bf16[32,1,2,4,2,16,128]{6,5,4,3,2,1,0:T(8,128)(2,1)}), bf16[32,1,2,4,2,16,128]{6,5,4,3,2,1,0:T(8,128)(2,1)}, u32[]{:S(2)}, u32[]{:S(2)}) %all-to-all-start.3) | async-done | bytes 2097184 | tf_op jit(solution)/shard_map/all_to_all | solution.py:297
  227.6 4.0 all-to-all-start.1
  231.6 46.8 %filter.6.f_ref = bf16[2,2,2048,1024]{3,2,1,0:T(8,128)(2,1)} custom-call(bf16[32,524288]{1,0:T(8,128)(2,1)} %x_ref.7, bf16[32,524288]{1,0:T(8,128)(2,1)} %x_ref.7, f32[16,8,2048]{2,1,0:T(8,128)} %jit_solution_.3.w_ref, bf16[32,1,2,4,2,16,128]{6,5,4,3,2,1,0:T(8,128)(2,1)} %copy-done), custom_call_target="tpu_custom_call" | custom-call | flops 134217728 | bytes 25165824 | tf_op jit(solution)/shard_map/filter/pallas_call | solution.py:122
  278.5 50.0 %dft.15 = bf16[32,4,2,4,2,16,128]{6,5,4,3,2,1,0:T(8,128)(2,1)} custom-call(bf16[2,2,2048,1024]{3,2,1,0:T(8,128)(2,1)} %filter.6.f_ref, bf16[4,2,256,1024]{3,2,1,0:T(8,128)(2,1)} %constant.12.clone.high_ref, bf16[4,2,256,1024]{3,2,1,0:T(8,128)(2,1)} %constant.13.clone.low_ref, bf16[32,1,2,4,2,16,128]{6,5,4,3,2,1,0:T(8,128)(2,1)} %all-to-all-done.3.rest_0_.refs_0_), custom_call_target="tpu_custom_call" | custom-call | flops 25769803776 | bytes 67108864 | tf_op jit(solution)/shard_map/dft/pallas_call | solution.py:177
  328.4 0.0 all-to-all-done.1.rest_0_.refs_0_
  328.4 0.0 copy-start.2
  328.4 1.3 copy-done.2
  329.8 6.0 all-to-all-start.5
  335.7 0.0 copy-start.6
  335.7 3.1 slice.3
  338.8 1.5 collective-permute-start
  340.3 4.7 collective-permute-done
  345.0 0.0 copy-done.6
  345.0 3.0 broadcast_select_fusion.halo_ref
  348.1 46.8 %filter.5.f_ref = bf16[2,2,2048,1024]{3,2,1,0:T(8,128)(2,1)} custom-call(bf16[32,524288]{1,0:T(8,128)(2,1)} %x_ref.7, bf16[32,30720]{1,0:T(8,128)(2,1)} %broadcast_select_fusion.halo_ref, f32[16,8,2048]{2,1,0:T(8,128)} %jit_solution_.3.w_ref, bf16[32,1,2,4,2,16,128]{6,5,4,3,2,1,0:T(8,128)(2,1)} %all-to-all-done.3.rest_0_.refs_0_), custom_call_target="tpu_custom_call" | custom-call | flops 134217728 | bytes 25165824 | tf_op jit(solution)/shard_map/filter/pallas_call | solution.py:122
  394.8 50.0 %dft.14 = bf16[32,4,2,4,2,16,128]{6,5,4,3,2,1,0:T(8,128)(2,1)} custom-call(bf16[2,2,2048,1024]{3,2,1,0:T(8,128)(2,1)} %filter.5.f_ref, bf16[4,2,256,1024]{3,2,1,0:T(8,128)(2,1)} %constant.12.clone.high_ref, bf16[4,2,256,1024]{3,2,1,0:T(8,128)(2,1)} %constant.13.clone.low_ref, bf16[32,1,2,4,2,16,128]{6,5,4,3,2,1,0:T(8,128)(2,1)} %copy-done.2), custom_call_target="tpu_custom_call" | custom-call | flops 25769803776 | bytes 67108864 | tf_op jit(solution)/shard_map/dft/pallas_call | solution.py:177
  444.8 77.0 %all-to-all-done.5.rest_0_.refs_2_ = bf16[32,4,2,4,2,16,128]{6,5,4,3,2,1,0:T(8,128)(2,1)} async-done(((bf16[32,4,2,4,2,16,128]{6,5,4,3,2,1,0:T(8,128)(2,1)}), bf16[32,4,2,4,2,16,128]{6,5,4,3,2,1,0:T(8,128)(2,1)}, u32[]{:S(2)}, u32[]{:S(2)}) %all-to-all-start.5) | async-done | bytes 8388640 | tf_op jit(solution)/shard_map/all_to_all | solution.py:297
  521.8 3.7 all-to-all-start.4
  525.5 46.8 %filter.7.f_ref = bf16[2,2,2048,1024]{3,2,1,0:T(8,128)(2,1)} custom-call(bf16[32,524288]{1,0:T(8,128)(2,1)} %x_ref.7, bf16[32,30720]{1,0:T(8,128)(2,1)} %broadcast_select_fusion.halo_ref, f32[16,8,2048]{2,1,0:T(8,128)} %jit_solution_.3.w_ref, bf16[32,1,2,4,2,16,128]{6,5,4,3,2,1,0:T(8,128)(2,1)} %copy-done.2), custom_call_target="tpu_custom_call" | custom-call | flops 134217728 | bytes 25165824 | tf_op jit(solution)/shard_map/filter/pallas_call | solution.py:122
  572.3 14.1 %dft.18 = bf16[32,1,2,4,2,16,128]{6,5,4,3,2,1,0:T(8,128)(2,1)} custom-call(bf16[2,2,2048,1024]{3,2,1,0:T(8,128)(2,1)} %filter.7.f_ref, bf16[4,2,256,1024]{3,2,1,0:T(8,128)(2,1)} %constant.12.clone.high_ref, bf16[4,2,256,1024]{3,2,1,0:T(8,128)(2,1)} %constant.13.clone.low_ref, bf16[32,4,2,4,2,16,128]{6,5,4,3,2,1,0:T(8,128)(2,1)} %all-to-all-done.5.rest_0_.refs_2_), custom_call_target="tpu_custom_call" | custom-call | flops 6442450944 | bytes 16777216 | tf_op jit(solution)/shard_map/dft/pallas_call | solution.py:177
  586.4 125.3 %all-to-all-done.4.rest_0_.refs_1_ = bf16[32,4,2,4,2,16,128]{6,5,4,3,2,1,0:T(8,128)(2,1)} async-done(((bf16[32,4,2,4,2,16,128]{6,5,4,3,2,1,0:T(8,128)(2,1)}), bf16[32,4,2,4,2,16,128]{6,5,4,3,2,1,0:T(8,128)(2,1)}, u32[]{:S(2)}, u32[]{:S(2)}) %all-to-all-start.4) | async-done | bytes 8388640 | tf_op jit(solution)/shard_map/all_to_all | solution.py:297
  711.6 2.7 all-to-all-start.8
  714.4 14.2 %dft.16 = bf16[32,1,2,4,2,16,128]{6,5,4,3,2,1,0:T(8,128)(2,1)} custom-call(bf16[2,2,2048,1024]{3,2,1,0:T(8,128)(2,1)} %filter.7.f_ref, bf16[4,2,256,1024]{3,2,1,0:T(8,128)(2,1)} %constant.12.clone.high_ref, bf16[4,2,256,1024]{3,2,1,0:T(8,128)(2,1)} %constant.13.clone.low_ref, bf16[32,4,2,4,2,16,128]{6,5,4,3,2,1,0:T(8,128)(2,1)} %all-to-all-done.4.rest_0_.refs_1_), custom_call_target="tpu_custom_call" | custom-call | flops 6442450944 | bytes 16777216 | tf_op jit(solution)/shard_map/dft/pallas_call | solution.py:177
  728.5 34.8 %all-to-all-done.8.rest_0_.refs_3_ = bf16[32,1,2,4,2,16,128]{6,5,4,3,2,1,0:T(8,128)(2,1)S(1)} async-done(((bf16[32,1,2,4,2,16,128]{6,5,4,3,2,1,0:T(8,128)(2,1)}), bf16[32,1,2,4,2,16,128]{6,5,4,3,2,1,0:T(8,128)(2,1)S(1)}, u32[]{:S(2)}, u32[]{:S(2)}) %all-to-all-start.8) | async-done | bytes 2097184 | tf_op jit(solution)/shard_map/all_to_all | solution.py:297
  763.3 0.0 copy-start.4
  763.3 1.4 copy-done.4
  764.7 3.9 all-to-all-start.6
  768.5 14.1 %dft.19 = bf16[32,1,2,4,2,16,128]{6,5,4,3,2,1,0:T(8,128)(2,1)} custom-call(bf16[2,2,2048,1024]{3,2,1,0:T(8,128)(2,1)} %filter.7.f_ref, bf16[4,2,256,1024]{3,2,1,0:T(8,128)(2,1)} %constant.12.clone.high_ref, bf16[4,2,256,1024]{3,2,1,0:T(8,128)(2,1)} %constant.13.clone.low_ref, bf16[32,1,2,4,2,16,128]{6,5,4,3,2,1,0:T(8,128)(2,1)} %copy-done.4), custom_call_target="tpu_custom_call" | custom-call | flops 6442450944 | bytes 16777216 | tf_op jit(solution)/shard_map/dft/pallas_call | solution.py:177
  782.6 34.8 %all-to-all-done.6.rest_0_.refs_3_ = bf16[32,1,2,4,2,16,128]{6,5,4,3,2,1,0:T(8,128)(2,1)S(1)} async-done(((bf16[32,1,2,4,2,16,128]{6,5,4,3,2,1,0:T(8,128)(2,1)}), bf16[32,1,2,4,2,16,128]{6,5,4,3,2,1,0:T(8,128)(2,1)S(1)}, u32[]{:S(2)}, u32[]{:S(2)}) %all-to-all-start.6) | async-done | bytes 2097184 | tf_op jit(solution)/shard_map/all_to_all | solution.py:297
  817.4 0.0 copy-start.1
  817.4 1.4 copy-done.1
  818.8 4.1 all-to-all-start.9
  823.0 14.1 %dft.17 = bf16[32,1,2,4,2,16,128]{6,5,4,3,2,1,0:T(8,128)(2,1)} custom-call(bf16[2,2,2048,1024]{3,2,1,0:T(8,128)(2,1)} %filter.7.f_ref, bf16[4,2,256,1024]{3,2,1,0:T(8,128)(2,1)} %constant.12.clone.high_ref, bf16[4,2,256,1024]{3,2,1,0:T(8,128)(2,1)} %constant.13.clone.low_ref, bf16[32,1,2,4,2,16,128]{6,5,4,3,2,1,0:T(8,128)(2,1)} %copy-done.1), custom_call_target="tpu_custom_call" | custom-call | flops 6442450944 | bytes 16777216 | tf_op jit(solution)/shard_map/dft/pallas_call | solution.py:177
  837.1 34.8 %all-to-all-done.9.refs_3_ = bf16[32,1,2,4,2,16,128]{6,5,4,3,2,1,0:T(8,128)(2,1)} async-done(((bf16[32,1,2,4,2,16,128]{6,5,4,3,2,1,0:T(8,128)(2,1)}), bf16[32,1,2,4,2,16,128]{6,5,4,3,2,1,0:T(8,128)(2,1)}, u32[]{:S(2)}, u32[]{:S(2)}) %all-to-all-start.9) | async-done | bytes 2097184 | tf_op jit(solution)/shard_map/all_to_all | solution.py:297
  871.9 4.2 all-to-all-start.7
  876.1 15.7 %gram.4.refs_4_ = f32[32,2,512,512]{3,2,1,0:T(8,128)} custom-call(bf16[32,1,2,4,2,16,128]{6,5,4,3,2,1,0:T(8,128)(2,1)} %copy-done.3, bf16[32,4,2,4,2,16,128]{6,5,4,3,2,1,0:T(8,128)(2,1)} %all-to-all-done.4.rest_0_.refs_1_, bf16[32,4,2,4,2,16,128]{6,5,4,3,2,1,0:T(8,128)(2,1)} %all-to-all-done.5.rest_0_.refs_2_, bf16[32,1,2,4,2,16,128]{6,5,4,3,2,1,0:T(8,128)(2,1)} %copy-done.4), custom_call_target="tpu_custom_call" | custom-call | flops 8589934592 | bytes 25165824 | tf_op jit(solution)/shard_map/gram/pallas_call | solution.py:247
  891.8 15.7 %gram.5.refs_4_ = f32[32,2,512,512]{3,2,1,0:T(8,128)} custom-call(bf16[32,1,2,4,2,16,128]{6,5,4,3,2,1,0:T(8,128)(2,1)} %copy-done, bf16[32,4,2,4,2,16,128]{6,5,4,3,2,1,0:T(8,128)(2,1)} %all-to-all-done.4.rest_0_.refs_1_, bf16[32,4,2,4,2,16,128]{6,5,4,3,2,1,0:T(8,128)(2,1)} %all-to-all-done.5.rest_0_.refs_2_, ...), custom_call_target="tpu_custom_call", output_to_operand_aliasing={{}: (4, {})} | custom-call | flops 8589934592 | bytes 25165824 | tf_op jit(solution)/shard_map/gram/pallas_call | solution.py:247
  907.4 15.7 %gram.6.refs_4_ = f32[32,2,512,512]{3,2,1,0:T(8,128)} custom-call(bf16[32,1,2,4,2,16,128]{6,5,4,3,2,1,0:T(8,128)(2,1)} %all-to-all-done.3.rest_0_.refs_0_, bf16[32,4,2,4,2,16,128]{6,5,4,3,2,1,0:T(8,128)(2,1)} %all-to-all-done.4.rest_0_.refs_1_, bf16[32,4,2,4,2,16,128]{6,5,4,3,2,1,0:T(8,128)(2,1)} %all-to-all-done.5.rest_0_.refs_2_, ...), custom_call_target="tpu_custom_call", output_to_operand_aliasing={{}: (4, {})} | custom-call | flops 8589934592 | bytes 25165824 | tf_op jit(solution)/shard_map/gram/pallas_call | solution.py:247
  923.1 1.8 all-to-all-done.7.refs_3_
  924.8 0.0 copy-start.5
  924.8 1.3 copy-done.5
  926.2 15.6 %gram.7 = f32[32,2,512,512]{3,2,1,0:T(8,128)} custom-call(bf16[32,1,2,4,2,16,128]{6,5,4,3,2,1,0:T(8,128)(2,1)} %copy-done.2, bf16[32,4,2,4,2,16,128]{6,5,4,3,2,1,0:T(8,128)(2,1)} %all-to-all-done.4.rest_0_.refs_1_, bf16[32,4,2,4,2,16,128]{6,5,4,3,2,1,0:T(8,128)(2,1)} %all-to-all-done.5.rest_0_.refs_2_, ...), custom_call_target="tpu_custom_call", output_to_operand_aliasing={{}: (4, {})} | custom-call | flops 8589934592 | bytes 25165824 | tf_op jit(solution)/shard_map/gram/pallas_call | solution.py:247
Async XLA Ops:
  62.8 56.2 %all-to-all-start.2 = ((bf16[32,1,2,4,2,16,128]{6,5,4,3,2,1,0:T(8,128)(2,1)}), bf16[32,1,2,4,2,16,128]{6,5,4,3,2,1,0:T(8,128)(2,1)S(1)}, u32[]{:S(2)}, u32[]{:S(2)}) async-start(bf16[32,1,2,4,2,16,128]{6,5,4,3,2,1,0:T(8,128)(2,1)} %dft.12), calls=%async_computation.2 | async-start | bytes 4194304 | tf_op jit(solution)/shard_map/all_to_all | solution.py:297
  119.0 1.3 copy-start.3
  120.4 52.9 %all-to-all-start = ((bf16[32,1,2,4,2,16,128]{6,5,4,3,2,1,0:T(8,128)(2,1)}), bf16[32,1,2,4,2,16,128]{6,5,4,3,2,1,0:T(8,128)(2,1)S(1)}, u32[]{:S(2)}, u32[]{:S(2)}) async-start(bf16[32,1,2,4,2,16,128]{6,5,4,3,2,1,0:T(8,128)(2,1)} %dft.10), calls=%async_computation | async-start | bytes 4194304 | tf_op jit(solution)/shard_map/all_to_all | solution.py:297
  173.3 1.3 copy-start
  174.6 53.0 %all-to-all-start.3 = ((bf16[32,1,2,4,2,16,128]{6,5,4,3,2,1,0:T(8,128)(2,1)}), bf16[32,1,2,4,2,16,128]{6,5,4,3,2,1,0:T(8,128)(2,1)}, u32[]{:S(2)}, u32[]{:S(2)}) async-start(bf16[32,1,2,4,2,16,128]{6,5,4,3,2,1,0:T(8,128)(2,1)} %dft.13), calls=%async_computation.3 | async-start | bytes 4194304 | tf_op jit(solution)/shard_map/all_to_all | solution.py:297
  227.6 100.8 %all-to-all-start.1 = ((bf16[32,1,2,4,2,16,128]{6,5,4,3,2,1,0:T(8,128)(2,1)}), bf16[32,1,2,4,2,16,128]{6,5,4,3,2,1,0:T(8,128)(2,1)S(1)}, u32[]{:S(2)}, u32[]{:S(2)}) async-start(bf16[32,1,2,4,2,16,128]{6,5,4,3,2,1,0:T(8,128)(2,1)} %dft.11), calls=%async_computation.1 | async-start | bytes 4194304 | tf_op jit(solution)/shard_map/all_to_all | solution.py:297
  328.4 1.3 copy-start.2
  329.8 192.0 %all-to-all-start.5 = ((bf16[32,4,2,4,2,16,128]{6,5,4,3,2,1,0:T(8,128)(2,1)}), bf16[32,4,2,4,2,16,128]{6,5,4,3,2,1,0:T(8,128)(2,1)}, u32[]{:S(2)}, u32[]{:S(2)}) async-start(bf16[32,4,2,4,2,16,128]{6,5,4,3,2,1,0:T(8,128)(2,1)} %dft.15), calls=%async_computation.5 | async-start | bytes 16777216 | tf_op jit(solution)/shard_map/all_to_all | solution.py:297
  335.7 9.3 copy-start.6
  338.8 6.2 collective-permute-start
  521.8 189.9 %all-to-all-start.4 = ((bf16[32,4,2,4,2,16,128]{6,5,4,3,2,1,0:T(8,128)(2,1)}), bf16[32,4,2,4,2,16,128]{6,5,4,3,2,1,0:T(8,128)(2,1)}, u32[]{:S(2)}, u32[]{:S(2)}) async-start(bf16[32,4,2,4,2,16,128]{6,5,4,3,2,1,0:T(8,128)(2,1)} %dft.14), calls=%async_computation.4 | async-start | bytes 16777216 | tf_op jit(solution)/shard_map/all_to_all | solution.py:297
  711.6 51.7 %all-to-all-start.8 = ((bf16[32,1,2,4,2,16,128]{6,5,4,3,2,1,0:T(8,128)(2,1)}), bf16[32,1,2,4,2,16,128]{6,5,4,3,2,1,0:T(8,128)(2,1)S(1)}, u32[]{:S(2)}, u32[]{:S(2)}) async-start(bf16[32,1,2,4,2,16,128]{6,5,4,3,2,1,0:T(8,128)(2,1)} %dft.18), calls=%async_computation.8 | async-start | bytes 4194304 | tf_op jit(solution)/shard_map/all_to_all | solution.py:297
  763.3 1.4 copy-start.4
  764.7 52.8 %all-to-all-start.6 = ((bf16[32,1,2,4,2,16,128]{6,5,4,3,2,1,0:T(8,128)(2,1)}), bf16[32,1,2,4,2,16,128]{6,5,4,3,2,1,0:T(8,128)(2,1)S(1)}, u32[]{:S(2)}, u32[]{:S(2)}) async-start(bf16[32,1,2,4,2,16,128]{6,5,4,3,2,1,0:T(8,128)(2,1)} %dft.16), calls=%async_computation.6 | async-start | bytes 4194304 | tf_op jit(solution)/shard_map/all_to_all | solution.py:297
  817.4 1.4 copy-start.1
  818.8 53.0 %all-to-all-start.9 = ((bf16[32,1,2,4,2,16,128]{6,5,4,3,2,1,0:T(8,128)(2,1)}), bf16[32,1,2,4,2,16,128]{6,5,4,3,2,1,0:T(8,128)(2,1)}, u32[]{:S(2)}, u32[]{:S(2)}) async-start(bf16[32,1,2,4,2,16,128]{6,5,4,3,2,1,0:T(8,128)(2,1)} %dft.19), calls=%async_computation.9 | async-start | bytes 4194304 | tf_op jit(solution)/shard_map/all_to_all | solution.py:297
  871.9 53.0 %all-to-all-start.7 = ((bf16[32,1,2,4,2,16,128]{6,5,4,3,2,1,0:T(8,128)(2,1)}), bf16[32,1,2,4,2,16,128]{6,5,4,3,2,1,0:T(8,128)(2,1)S(1)}, u32[]{:S(2)}, u32[]{:S(2)}) async-start(bf16[32,1,2,4,2,16,128]{6,5,4,3,2,1,0:T(8,128)(2,1)} %dft.17), calls=%async_computation.7 | async-start | bytes 4194304 | tf_op jit(solution)/shard_map/all_to_all | solution.py:297
  924.8 1.3 copy-start.5

commit v2 on v1

v2 whole, which is shorter than its diff:
```python
import functools
import math

import jax
import jax.numpy as jnp
import ml_dtypes
import numpy as np
from jax import lax
from jax.experimental import pallas as pl
from jax.experimental.pallas import tpu as pltpu
from jax.sharding import PartitionSpec as P

FFT_LEN = 2048
CHANNELS = 1024
TAPS = 16
FOLD = FFT_LEN // 2
SPAN = 128
GROUPS = 4
BATCH = 8
STRETCH = 32
COLS = 256
VMEM = 127 * 512 * 1024
AXES = ("wide", "narrow")


def odd_stride(rows):
    return rows + 8 * (1 - rows // 8 % 2)


def pfb_window():
    n = np.arange(TAPS * FFT_LEN, dtype=np.float64)
    total = TAPS * FFT_LEN
    taper = 0.5 - 0.5 * np.cos(2.0 * np.pi * (n + 0.5) / total)
    window = np.sinc((n + 0.5 - total / 2) / FFT_LEN) * taper
    return window.astype(np.float32).reshape(TAPS, FFT_LEN)


def split16(values):
    high = values.astype(ml_dtypes.bfloat16)
    low = (values - high.astype(np.float64)).astype(ml_dtypes.bfloat16)
    return high, low


def dft_table(n_dev):
    chan_dev = CHANNELS // n_dev
    cg = chan_dev // GROUPS
    g, p, d, h = np.meshgrid(
        np.arange(GROUPS), np.arange(2), np.arange(n_dev), np.arange(cg // 2), indexing="ij"
    )
    chan = d * chan_dev + g * cg + 2 * h + p
    turns = chan[..., None] * np.arange(FOLD) % FFT_LEN
    angles = 2.0 * np.pi * turns / FFT_LEN
    table = np.stack([np.cos(angles), -np.sin(angles)], axis=-2) / math.sqrt(FFT_LEN)
    return np.concatenate(split16(table.reshape(GROUPS, 2, CHANNELS // GROUPS, FOLD)), axis=2)


def filter_kernel(first, n_in, with_after, x_ref, w_ref, halo_ref, *rest):
    outs, (even_ref, odd_ref, tail_ref) = rest[-7:-3], rest[-3:]
    n_rows = x_ref.shape[0]
    pitch = odd_stride(STRETCH)
    halo_len = (TAPS - 1) * FFT_LEN
    if with_after:
        is_last = pl.program_id(0) == pl.num_programs(0) - 1

        @pl.when(is_last)
        def _():
            tail_ref[...] = rest[0][:, :halo_len]

        @pl.when(jnp.logical_not(is_last))
        def _():
            tail_ref[...] = halo_ref[:, :halo_len]

        next_ref = tail_ref
    else:
        next_ref = halo_ref

    def load(t, k):
        ref, at = (x_ref, t) if t < STRETCH else (next_ref, t - STRETCH)
        tile = ref[:, pl.ds(pl.multiple_of(at * FFT_LEN + k, 128), 128)].astype(jnp.float32)
        return tile.reshape(n_rows // 8, 8, 128)[first // 8 : (first + n_in) // 8]

    def fir(m0, k):
        weights = [w_ref[p, :, pl.ds(pl.multiple_of(k, 128), 128)][None] for p in range(TAPS)]
        sums = [None] * BATCH
        for t in range(BATCH + TAPS - 1):
            tile = load(m0 + t, k)
            for j in range(max(0, t - TAPS + 1), min(BATCH, t + 1)):
                term = weights[t - j] * tile
                sums[j] = term if sums[j] is None else sums[j] + term
        return sums

    def columns(kt, _):
        k = kt * 128
        for m0 in range(0, STRETCH, BATCH):
            lower, upper = fir(m0, k), fir(m0, k + FOLD)
            for j in range(BATCH):
                rows = pl.ds(m0 + j, n_in, stride=pitch)
                even_ref[rows, :] = (lower[j] + upper[j]).reshape(n_in, 128)
                odd_ref[rows, :] = (lower[j] - upper[j]).reshape(n_in, 128)
        chunk, at = kt // (COLS // 128), pl.ds(pl.multiple_of(kt % (COLS // 128) * 128, 128), 128)
        for i in range(n_in):
            for p, ref in ((0, even_ref), (1, odd_ref)):
                value = ref[pl.ds(i * pitch, STRETCH), :]
                high = value.astype(jnp.bfloat16)
                low = (value - high.astype(jnp.float32)).astype(jnp.bfloat16)
                outs[2 * p][chunk, i, :, at] = high
                outs[2 * p + 1][chunk, i, :, at] = low
        return 0

    lax.fori_loop(0, FOLD // 128, columns, 0)


def filter_unit(voltages, after, weights, start, n_in, half, halves, deps):
    n_block = min(16, voltages.shape[0])
    ig = start // n_block
    steps = SPAN // STRETCH
    scale = STRETCH // TAPS
    last_halo = voltages.shape[1] // (TAPS * FFT_LEN) - 1
    with_after = half == halves - 1

    def halo_at(t):
        return (ig, jnp.minimum((half * steps + t + 1) * scale, last_halo))

    args = [voltages, weights, voltages]
    specs = [
        pl.BlockSpec((n_block, STRETCH * FFT_LEN), lambda t: (ig, half * steps + t)),
        pl.BlockSpec((TAPS, 8, FFT_LEN), lambda t: (0, 0, 0)),
        pl.BlockSpec((n_block, TAPS * FFT_LEN), halo_at),
    ]
    if with_after:
        args.append(after)
        specs.append(pl.BlockSpec((n_block, after.shape[1]), lambda t: (ig, 0)))
    rows = n_in * SPAN
    out_shape = (FOLD // COLS, n_in, SPAN, COLS)
    folded = pl.pallas_call(
        functools.partial(filter_kernel, start % n_block, n_in, with_after),
        grid=(steps,),
        in_specs=specs + [pl.BlockSpec(memory_space=pl.ANY)] * len(deps),
        out_specs=[pl.BlockSpec((FOLD // COLS, n_in, STRETCH, COLS), lambda t: (0, 0, t, 0))] * 4,
        out_shape=[jax.ShapeDtypeStruct(out_shape, jnp.bfloat16)] * 4,
        scratch_shapes=[
            pltpu.VMEM((n_in * odd_stride(STRETCH), 128), jnp.float32),
            pltpu.VMEM((n_in * odd_stride(STRETCH), 128), jnp.float32),
            pltpu.VMEM((n_block, (TAPS - 1) * FFT_LEN), jnp.bfloat16),
        ],
        compiler_params=pltpu.CompilerParams(vmem_limit_bytes=VMEM),
        cost_estimate=pl.CostEstimate(
            flops=rows * FFT_LEN * TAPS * 2, bytes_accessed=rows * FFT_LEN * 6, transcendentals=0
        ),
        name="filter",
    )(*args, *deps)
    return [f.reshape(FOLD // COLS, rows, COLS) for f in folded]


def dft_kernel(*refs):
    folded, table_ref, (out_ref, held_ref) = refs[:4], refs[4], refs[-2:]
    step = pl.program_id(1)
    n_in = out_ref.shape[-2]
    n_rows = table_ref.shape[2] // 2
    pitch = odd_stride(n_in)
    n_chunks, f_rows, _ = folded[0].shape
    n_here = f_rows // SPAN

    def product(p, low_too, chunk, ref, rows):
        left = table_ref[0, p, : (1 + low_too) * n_rows, chunk * COLS : (chunk + 1) * COLS]
        dims = (((1,), (1,)), ((), ()))
        return lax.dot_general(left, ref[chunk, rows, :], dims, preferred_element_type=jnp.float32)

    for p in range(2):
        for pair in range(0, n_here, 2):
            take = min(2, n_here - pair)
            rows = pl.ds(pair * SPAN, take * SPAN)
            both = sum(product(p, 1, chunk, folded[2 * p], rows) for chunk in range(n_chunks))
            rest = sum(product(p, 0, chunk, folded[2 * p + 1], rows) for chunk in range(n_chunks))
            total = both[:n_rows] + (both[n_rows:] + rest)
            for j in range(take):
                at = step * n_here + pair + j
                held_ref[p, pl.ds(at, n_rows, stride=pitch), :] = total[:, j * SPAN : (j + 1) * SPAN]

    @pl.when(step == pl.num_programs(1) - 1)
    def _():
        n_dev, _, _, n_pair, _, _, _ = out_ref.shape
        for p in range(2):
            for d in range(n_dev):
                each = n_pair * 2 * pitch
                block = held_ref[p, pl.ds(d * each, each), :].reshape(n_pair, 2, pitch, SPAN)
                out_ref[d, 0, p] = block[:, :, :n_in].astype(jnp.bfloat16)


def dft_unit(folded, table, n_dev, n_in, g0, n_groups, n_slots, slot, previous, deps):
    chan_dev = CHANNELS // n_dev
    n_pair = chan_dev // GROUPS // 2
    n_rows = CHANNELS // GROUPS
    here = min(4, n_in)
    filled = [] if previous is None else [previous]
    f_block = (FOLD // COLS, here * SPAN, COLS)
    return pl.pallas_call(
        dft_kernel,
        grid=(n_groups, n_in // here),
        in_specs=[pl.BlockSpec(f_block, lambda g, i: (0, i, 0))] * 4
        + [pl.BlockSpec((1, 2, 2 * n_rows, FOLD), lambda g, i: (g0 + g, 0, 0, 0))]
        + [pl.BlockSpec(memory_space=pl.ANY)] * (len(deps) + len(filled)),
        out_specs=pl.BlockSpec(
            (n_dev, 1, 2, n_pair, 2, n_in, SPAN), lambda g, i: (0, slot + g, 0, 0, 0, 0, 0)
        ),
        out_shape=jax.ShapeDtypeStruct(
            (n_dev, n_slots, 2, n_pair, 2, n_in, SPAN), jnp.bfloat16
        ),
        input_output_aliases={5: 0} if filled else {},
        scratch_shapes=[pltpu.VMEM((2, n_rows * odd_stride(n_in), SPAN), jnp.float32)],
        compiler_params=pltpu.CompilerParams(vmem_limit_bytes=VMEM),
        cost_estimate=pl.CostEstimate(
            flops=n_groups * 12 * n_rows * n_in * SPAN * FOLD,
            bytes_accessed=n_groups * n_in * SPAN * FOLD * 8,
            transcendentals=0,
        ),
        name="dft",
    )(*folded, table, *filled, *deps)


def gram_kernel(layout, halves, n_wide, n_narrow, time_len, first, *refs):
    units = refs[: len(layout)]
    out_ref, both_ref, slot_ref, sems = refs[-4:]
    step, steps = pl.program_id(0), pl.num_programs(0)
    local_inputs = out_ref.shape[2] // n_wide

    def send(at, p, part):
        slot = lax.rem(at, 2)
        return pltpu.make_async_copy(
            slot_ref.at[slot, p, part], out_ref.at[first + 2 * at + p, part], sems.at[slot, p, part]
        )

    def wait_all(at):
        for p in range(2):
            for part in range(2):
                send(at, p, part).wait()

    @pl.when(step >= 2)
    def _():
        wait_all(step - 2)

    for p in range(2):
        for w in range(n_wide):
            for n in range(n_narrow):
                for unit, (start, n_in, half) in zip(units, layout):
                    row = pl.ds(w * local_inputs + start, n_in)
                    at = (n * halves + half) * SPAN
                    for part in range(2):
                        both_ref[p, row, pl.ds(part * time_len + at, SPAN)] = unit[
                            w * n_narrow + n, 0, p, 0, part
                        ]

    def product(left, right):
        dims = (((1,), (1,)), ((), ()))
        return lax.dot_general(left, right, dims, preferred_element_type=jnp.float32)

    scale = 1.0 / time_len
    for p in range(2):
        both, real, imag = both_ref[p], both_ref[p, :, :time_len], both_ref[p, :, time_len:]
        slot_ref[lax.rem(step, 2), p, 0] = product(both, both) * scale
        send(step, p, 0).start()
        cross = product(imag, real) * scale
        slot_ref[lax.rem(step, 2), p, 1] = cross - cross.T
        send(step, p, 1).start()

    @pl.when(step == steps - 1)
    def _():
        @pl.when(step >= 1)
        def _():
            wait_all(step - 1)

        wait_all(step)


def gram_group(units, layout, places, previous, n_wide, n_narrow, halves, inputs, group):
    n_dev = n_wide * n_narrow
    chan_dev = CHANNELS // n_dev
    cg = chan_dev // GROUPS
    n_units = len(units)
    time_len = n_narrow * halves * SPAN
    specs = [
        pl.BlockSpec(
            (n_dev, 1, 2, 1, 2, n_in, SPAN), lambda t, at=at: (0, at, 0, t, 0, 0, 0)
        )
        for at, (_, n_in, _) in zip(places, layout)
    ]
    args = list(units)
    aliases = {}
    if previous is not None:
        specs.append(pl.BlockSpec(memory_space=pl.ANY))
        args.append(previous)
        aliases = {n_units: 0}
    return pl.pallas_call(
        functools.partial(gram_kernel, layout, halves, n_wide, n_narrow, time_len, group * cg),
        grid=(cg // 2,),
        in_specs=specs,
        out_specs=pl.BlockSpec(memory_space=pl.ANY),
        out_shape=jax.ShapeDtypeStruct((chan_dev, 2, inputs, inputs), jnp.float32),
        scratch_shapes=[
            pltpu.VMEM((2, inputs, 2 * time_len), jnp.bfloat16),
            pltpu.VMEM((2, 2, 2, inputs, inputs), jnp.float32),
            pltpu.SemaphoreType.DMA((2, 2, 2)),
        ],
        input_output_aliases=aliases,
        compiler_params=pltpu.CompilerParams(vmem_limit_bytes=VMEM),
        cost_estimate=pl.CostEstimate(
            flops=cg * 8 * inputs * inputs * time_len,
            bytes_accessed=cg * inputs * (8 * inputs + 4 * time_len),
            transcendentals=0,
        ),
        name="gram",
    )(*args)


def shards(voltages, following):
    n_wide, n_narrow = lax.axis_size("wide"), lax.axis_size("narrow")
    n_dev = n_wide * n_narrow
    local_inputs, local_span = voltages.shape
    halves = local_span // (SPAN * FFT_LEN)

    leading = voltages[:, : (TAPS - 1) * FFT_LEN]
    shifted = lax.ppermute(leading, "narrow", [(i, i - 1) for i in range(1, n_narrow)])
    is_final = lax.axis_index("narrow") == n_narrow - 1
    after = jnp.where(is_final, following, shifted)

    table = jnp.asarray(dft_table(n_dev))
    weights = np.broadcast_to(pfb_window()[:, None, :], (TAPS, 8, FFT_LEN))
    weights = jnp.asarray(np.ascontiguousarray(weights))

    n_unit = min(16, local_inputs)
    layout = [
        (start, n_unit, half)
        for half in range(halves)
        for start in range(0, local_inputs, n_unit)
    ]
    if n_unit == 16:
        layout[:1] = [(0, 8, 0), (8, 8, 0)]
    last = len(layout) - 1
    parts = [[(0, 0, 1)], [(0, 1, GROUPS - 1)]]
    parts += [[(index, 0, GROUPS)] for index in range(1, last - 1)]
    parts += [[(last - 1, 0, GROUPS)]] if last > 1 else []
    parts[-1:] = [parts[-1] + [(last, 0, GROUPS - 1)]] if last > 1 else [parts[-1], [(last, 0, GROUPS - 1)]]
    parts += [[(last, GROUPS - 1, 1)]]

    received = []
    folded = {}
    place = {}
    for job, pieces in enumerate(parts):
        deps = [received[job - 2]] if job >= 2 else []
        n_slots = sum(size for _, _, size in pieces)
        spectra, slot = None, 0
        for index, first, size in pieces:
            start, n_in, half = layout[index]
            if index not in folded:
                folded[index] = filter_unit(
                    voltages, after, weights, start, n_in, half, halves, deps
                )
            spectra = dft_unit(
                folded[index], table, n_dev, n_in, first, size, n_slots, slot, spectra, deps
            )
            for group in range(first, first + size):
                place[index, group] = (job, slot + group - first)
            slot += size
        received.append(lax.all_to_all(spectra, AXES, split_axis=0, concat_axis=0, tiled=True))

    result = None
    for group in range(GROUPS):
        found = [place[index, group] for index in range(len(layout))]
        units = [received[job] for job, _ in found]
        places = [slot for _, slot in found]
        result = gram_group(
            units, layout, places, result, n_wide, n_narrow, halves, n_wide * local_inputs, group
        )
    return result


def solution(mesh):
    in_specs = (P("wide", "narrow"), P("wide", None))
    out_specs = P(("wide", "narrow"), None, None, None)
    return jax.shard_map(shards, mesh=mesh, in_specs=in_specs, out_specs=out_specs, check_vma=False)
```

time: 946 us -> 815 us (0.86)
  Pallas kernels: 462 us -> 331 us
  waiting for transfers between devices: 418 us -> 449 us
  starting transfers between devices: 45.6 us -> 28.3 us
  local copies, waits for them, and re-layouts: 13.1 us -> 3.09 us
    pallas_call x18 -> x16, Pallas kernels: 462 us -> 331 us  [the longest x7 169 us: dft_unit(): pl.pallas_call(dft_kernel, grid=(n_groups, n_in // here), in_specs=[pl.Bl...]
    all_to_all x10 -> x6, waiting for transfers between devices: 413 us -> 444 us  [shards(): lax.all_to_all(spectra, AXES, split_axis=0, concat_axis=0, tiled=True)]
    all_to_all x10 -> x6, starting transfers between devices: 44.1 us -> 26.9 us  [shards(): lax.all_to_all(spectra, AXES, split_axis=0, concat_axis=0, tiled=True)]
  transfers between devices with their start and end apart: 11 -> 7, of which waited for: 10 -> 7; matrix products, arithmetic and copies ran while one was open for 1% -> 1% of each run, Pallas kernels for 41% -> 36%
where the time goes in v2:
time: 815 us; the launch traced here: 814 us
  waiting for transfers between devices  449 us (55%)
  Pallas kernels  331 us (41%)
  starting transfers between devices  28.3 us (3%)
    all_to_all x6, waiting for transfers between devices, shards(): lax.all_to_all(spectra, AXES, split_axis=0, concat_axis=0, tiled=True)  444 us
    pallas_call x7, Pallas kernels, dft_unit(): pl.pallas_call(dft_kernel, grid=(n_groups, n_in // here), in_specs=[pl.Bl...  169 us
    pallas_call x5, Pallas kernels, filter_unit(): pl.pallas_call(functools.partial(filter_kernel, start % n_block, n_in, wi...  115 us
    pallas_call x4, Pallas kernels, gram_group(): pl.pallas_call(functools.partial(gram_kernel, layout, halves, n_wide, n_n...  46.9 us
    all_to_all x6, starting transfers between devices, shards(): lax.all_to_all(spectra, AXES, split_axis=0, concat_axis=0, tiled=True)  26.9 us
  transfers between devices with their start and end apart: 7, of which 7 were waited for; matrix products, arithmetic and copies ran while one was open for 1% of the time, Pallas kernels for 36%

profile of v2, /device:TPU:0, one launch (start us, length us, event | category | flops | bytes accessed | tf_op | source)
XLA Modules:
  0.0 814.2 jit_solution(3048922200720168904)
XLA Ops:
  0.0 15.2 %filter.5 = (bf16[4,8,128,256]{3,2,1,0:T(8,128)(2,1)}, bf16[4,8,128,256]{3,2,1,0:T(8,128)(2,1)}, bf16[4,8,128,256]{3,2,1,0:T(8,128)(2,1)}, bf16[4,8,128,256]{3,2,1,0:T(8,128)(2,1)}) custom-call(bf16[32,524288]{1,0:T(8,128)(2,1)} %halo_ref.9, f32[16,8,2048]{2,1,0:T(8,128)} %constant.11.clone.w_ref, bf16[32,524288]{1,0:T(8,128)(2,1)} %halo_ref.9), custom_call_target="tpu_custom_call" | custom-call | flops 67108864 | bytes 12582912 | tf_op jit(solution)/shard_map/filter/pallas_call | solution.py:135
  15.2 7.7 dft.8
  22.9 7.4 all-to-all-start.1
  30.4 17.2 %dft.7 = bf16[32,3,2,4,2,8,128]{6,5,4,3,2,1,0:T(8,128)(2,1)} custom-call(bf16[4,1024,256]{2,1,0:T(8,128)(2,1)} %bitcast.29, bf16[4,1024,256]{2,1,0:T(8,128)(2,1)} %bitcast.31, bf16[4,1024,256]{2,1,0:T(8,128)(2,1)} %bitcast.33, bf16[4,1024,256]{2,1,0:T(8,128)(2,1)} %bitcast.35, bf16[4,2,512,1024]{3,2,1,0:T(8,128)(2,1)} %constant.10.clone.refs_4_), custom_call_target="tpu_custom_call" | custom-call | flops 9663676416 | bytes 25165824 | tf_op jit(solution)/shard_map/dft/pallas_call | solution.py:197
  47.6 9.0 %all-to-all-done.1.rest_0_.refs_5_.refs_0_ = bf16[32,1,2,4,2,8,128]{6,5,4,3,2,1,0:T(8,128)(2,1)} async-done(((bf16[32,1,2,4,2,8,128]{6,5,4,3,2,1,0:T(8,128)(2,1)}), bf16[32,1,2,4,2,8,128]{6,5,4,3,2,1,0:T(8,128)(2,1)}, u32[]{:S(2)}, u32[]{:S(2)}) %all-to-all-start.1) | async-done | bytes 1048608 | tf_op jit(solution)/shard_map/all_to_all | solution.py:364
  56.6 3.7 all-to-all-start
  60.3 15.3 %filter.6 = (bf16[4,8,128,256]{3,2,1,0:T(8,128)(2,1)}, bf16[4,8,128,256]{3,2,1,0:T(8,128)(2,1)}, bf16[4,8,128,256]{3,2,1,0:T(8,128)(2,1)}, bf16[4,8,128,256]{3,2,1,0:T(8,128)(2,1)}) custom-call(bf16[32,524288]{1,0:T(8,128)(2,1)} %halo_ref.9, f32[16,8,2048]{2,1,0:T(8,128)} %constant.11.clone.w_ref, bf16[32,524288]{1,0:T(8,128)(2,1)} %halo_ref.9, ...), custom_call_target="tpu_custom_call" | custom-call | flops 67108864 | bytes 12582912 | tf_op jit(solution)/shard_map/filter/pallas_call | solution.py:135
  75.6 21.9 %dft.9 = bf16[32,4,2,4,2,8,128]{6,5,4,3,2,1,0:T(8,128)(2,1)} custom-call(bf16[4,1024,256]{2,1,0:T(8,128)(2,1)} %bitcast.44, bf16[4,1024,256]{2,1,0:T(8,128)(2,1)} %bitcast.45, bf16[4,1024,256]{2,1,0:T(8,128)(2,1)} %bitcast.46, bf16[4,1024,256]{2,1,0:T(8,128)(2,1)} %bitcast.47, bf16[4,2,512,1024]{3,2,1,0:T(8,128)(2,1)} %constant.10.clone.refs_4_, ...), custom_call_target="tpu_custom_call" | custom-call | flops 12884901888 | bytes 33554432 | tf_op jit(solution)/shard_map/dft/pallas_call | solution.py:197
  97.5 34.3 %all-to-all-done.rest_0_.refs_5_.refs_0_ = bf16[32,3,2,4,2,8,128]{6,5,4,3,2,1,0:T(8,128)(2,1)} async-done(((bf16[32,3,2,4,2,8,128]{6,5,4,3,2,1,0:T(8,128)(2,1)}), bf16[32,3,2,4,2,8,128]{6,5,4,3,2,1,0:T(8,128)(2,1)}, u32[]{:S(2)}, u32[]{:S(2)}) %all-to-all-start) | async-done | bytes 3145760 | tf_op jit(solution)/shard_map/all_to_all | solution.py:364
  131.8 4.1 all-to-all-start.2
  135.9 27.7 %filter.7 = (bf16[4,16,128,256]{3,2,1,0:T(8,128)(2,1)}, bf16[4,16,128,256]{3,2,1,0:T(8,128)(2,1)}, bf16[4,16,128,256]{3,2,1,0:T(8,128)(2,1)}, bf16[4,16,128,256]{3,2,1,0:T(8,128)(2,1)}) custom-call(bf16[32,524288]{1,0:T(8,128)(2,1)} %halo_ref.9, f32[16,8,2048]{2,1,0:T(8,128)} %constant.11.clone.w_ref, bf16[32,524288]{1,0:T(8,128)(2,1)} %halo_ref.9, ...), custom_call_target="tpu_custom_call" | custom-call | flops 134217728 | bytes 25165824 | tf_op jit(solution)/shard_map/filter/pallas_call | solution.py:135
  163.6 39.8 %dft.10 = bf16[32,4,2,4,2,16,128]{6,5,4,3,2,1,0:T(8,128)(2,1)} custom-call(bf16[4,2048,256]{2,1,0:T(8,128)(2,1)} %bitcast.40, bf16[4,2048,256]{2,1,0:T(8,128)(2,1)} %bitcast.41, bf16[4,2048,256]{2,1,0:T(8,128)(2,1)} %bitcast.42, bf16[4,2048,256]{2,1,0:T(8,128)(2,1)} %bitcast.43, bf16[4,2,512,1024]{3,2,1,0:T(8,128)(2,1)} %constant.10.clone.refs_4_, ...), custom_call_target="tpu_custom_call" | custom-call | flops 25769803776 | bytes 67108864 | tf_op jit(solution)/shard_map/dft/pallas_call | solution.py:197
  203.3 26.4 %all-to-all-done.2.rest_1_.refs_5_.refs_6_.refs_1_ = bf16[32,4,2,4,2,8,128]{6,5,4,3,2,1,0:T(8,128)(2,1)} async-done(((bf16[32,4,2,4,2,8,128]{6,5,4,3,2,1,0:T(8,128)(2,1)}), bf16[32,4,2,4,2,8,128]{6,5,4,3,2,1,0:T(8,128)(2,1)}, u32[]{:S(2)}, u32[]{:S(2)}) %all-to-all-start.2) | async-done | bytes 4194336 | tf_op jit(solution)/shard_map/all_to_all | solution.py:364
  229.7 4.1 all-to-all-start.3
  233.8 0.0 copy-start
  233.8 3.1 slice.3
  236.9 1.5 collective-permute-start
  238.4 4.7 collective-permute-done
  243.1 0.0 copy-done
  243.1 3.0 broadcast_select_fusion.rest_0_
  246.1 28.2 %filter.9 = (bf16[4,16,128,256]{3,2,1,0:T(8,128)(2,1)}, bf16[4,16,128,256]{3,2,1,0:T(8,128)(2,1)}, bf16[4,16,128,256]{3,2,1,0:T(8,128)(2,1)}, bf16[4,16,128,256]{3,2,1,0:T(8,128)(2,1)}) custom-call(bf16[32,524288]{1,0:T(8,128)(2,1)} %halo_ref.9, f32[16,8,2048]{2,1,0:T(8,128)} %constant.11.clone.w_ref, bf16[32,524288]{1,0:T(8,128)(2,1)} %halo_ref.9, ...), custom_call_target="tpu_custom_call" | custom-call | flops 134217728 | bytes 25165824 | tf_op jit(solution)/shard_map/filter/pallas_call | solution.py:135
  274.4 28.2 %filter.8 = (bf16[4,16,128,256]{3,2,1,0:T(8,128)(2,1)}, bf16[4,16,128,256]{3,2,1,0:T(8,128)(2,1)}, bf16[4,16,128,256]{3,2,1,0:T(8,128)(2,1)}, bf16[4,16,128,256]{3,2,1,0:T(8,128)(2,1)}) custom-call(bf16[32,524288]{1,0:T(8,128)(2,1)} %halo_ref.9, f32[16,8,2048]{2,1,0:T(8,128)} %constant.11.clone.w_ref, bf16[32,524288]{1,0:T(8,128)(2,1)} %halo_ref.9, ...), custom_call_target="tpu_custom_call" | custom-call | flops 134217728 | bytes 25165824 | tf_op jit(solution)/shard_map/filter/pallas_call | solution.py:135
  302.6 39.8 %dft.11.refs_5_ = bf16[32,7,2,4,2,16,128]{6,5,4,3,2,1,0:T(8,128)(2,1)} custom-call(bf16[4,2048,256]{2,1,0:T(8,128)(2,1)} %bitcast.36, bf16[4,2048,256]{2,1,0:T(8,128)(2,1)} %bitcast.37, bf16[4,2048,256]{2,1,0:T(8,128)(2,1)} %bitcast.38, bf16[4,2048,256]{2,1,0:T(8,128)(2,1)} %bitcast.39, bf16[4,2,512,1024]{3,2,1,0:T(8,128)(2,1)} %constant.10.clone.refs_4_, ...), custom_call_target="tpu_custom_call" | custom-call | flops 25769803776 | bytes 67108864 | tf_op jit(solution)/shard_map/dft/pallas_call | solution.py:197
  342.4 30.6 %dft.12 = bf16[32,7,2,4,2,16,128]{6,5,4,3,2,1,0:T(8,128)(2,1)} custom-call(bf16[4,2048,256]{2,1,0:T(8,128)(2,1)} %bitcast.20, bf16[4,2048,256]{2,1,0:T(8,128)(2,1)} %bitcast.22, bf16[4,2048,256]{2,1,0:T(8,128)(2,1)} %bitcast.24, bf16[4,2048,256]{2,1,0:T(8,128)(2,1)} %bitcast.26, ...), custom_call_target="tpu_custom_call", output_to_operand_aliasing={{}: (5, {})} | custom-call | flops 19327352832 | bytes 50331648 | tf_op jit(solution)/shard_map/dft/pallas_call | solution.py:197
  373.0 46.9 %all-to-all-done.3.refs_5_.refs_2_ = bf16[32,4,2,4,2,16,128]{6,5,4,3,2,1,0:T(8,128)(2,1)} async-done(((bf16[32,4,2,4,2,16,128]{6,5,4,3,2,1,0:T(8,128)(2,1)}), bf16[32,4,2,4,2,16,128]{6,5,4,3,2,1,0:T(8,128)(2,1)}, u32[]{:S(2)}, u32[]{:S(2)}) %all-to-all-start.3) | async-done | bytes 8388640 | tf_op jit(solution)/shard_map/all_to_all | solution.py:364
  419.9 3.8 all-to-all-start.4
  423.7 12.2 %dft.13 = bf16[32,1,2,4,2,16,128]{6,5,4,3,2,1,0:T(8,128)(2,1)} custom-call(bf16[4,2048,256]{2,1,0:T(8,128)(2,1)} %bitcast.21, bf16[4,2048,256]{2,1,0:T(8,128)(2,1)} %bitcast.23, bf16[4,2048,256]{2,1,0:T(8,128)(2,1)} %bitcast.25, bf16[4,2048,256]{2,1,0:T(8,128)(2,1)} %bitcast.27, bf16[4,2,512,1024]{3,2,1,0:T(8,128)(2,1)} %constant.10.clone.refs_4_, ...), custom_call_target="tpu_custom_call" | custom-call | flops 6442450944 | bytes 16777216 | tf_op jit(solution)/shard_map/dft/pallas_call | solution.py:197
  435.9 313.7 %all-to-all-done.4.refs_3_.refs_4_ = bf16[32,7,2,4,2,16,128]{6,5,4,3,2,1,0:T(8,128)(2,1)} async-done(((bf16[32,7,2,4,2,16,128]{6,5,4,3,2,1,0:T(8,128)(2,1)}), bf16[32,7,2,4,2,16,128]{6,5,4,3,2,1,0:T(8,128)(2,1)}, u32[]{:S(2)}, u32[]{:S(2)}) %all-to-all-start.4) | async-done | bytes 14680096 | tf_op jit(solution)/shard_map/all_to_all | solution.py:364
  749.7 3.7 all-to-all-start.5
  753.4 11.7 %gram.4.refs_5_ = f32[32,2,512,512]{3,2,1,0:T(8,128)} custom-call(bf16[32,1,2,4,2,8,128]{6,5,4,3,2,1,0:T(8,128)(2,1)} %all-to-all-done.1.rest_0_.refs_5_.refs_0_, bf16[32,4,2,4,2,8,128]{6,5,4,3,2,1,0:T(8,128)(2,1)} %all-to-all-done.2.rest_1_.refs_5_.refs_6_.refs_1_, bf16[32,4,2,4,2,16,128]{6,5,4,3,2,1,0:T(8,128)(2,1)} %all-to-all-done.3.refs_5_.refs_2_, ...), custom_call_target="tpu_custom_call" | custom-call | flops 8589934592 | bytes 25165824 | tf_op jit(solution)/shard_map/gram/pallas_call | solution.py:293
  765.1 11.7 %gram.5.refs_5_ = f32[32,2,512,512]{3,2,1,0:T(8,128)} custom-call(bf16[32,3,2,4,2,8,128]{6,5,4,3,2,1,0:T(8,128)(2,1)} %all-to-all-done.rest_0_.refs_5_.refs_0_, bf16[32,4,2,4,2,8,128]{6,5,4,3,2,1,0:T(8,128)(2,1)} %all-to-all-done.2.rest_1_.refs_5_.refs_6_.refs_1_, ...), custom_call_target="tpu_custom_call", output_to_operand_aliasing={{}: (5, {})} | custom-call | flops 8589934592 | bytes 25165824 | tf_op jit(solution)/shard_map/gram/pallas_call | solution.py:293
  776.9 11.7 %gram.6.refs_5_ = f32[32,2,512,512]{3,2,1,0:T(8,128)} custom-call(bf16[32,3,2,4,2,8,128]{6,5,4,3,2,1,0:T(8,128)(2,1)} %all-to-all-done.rest_0_.refs_5_.refs_0_, bf16[32,4,2,4,2,8,128]{6,5,4,3,2,1,0:T(8,128)(2,1)} %all-to-all-done.2.rest_1_.refs_5_.refs_6_.refs_1_, ...), custom_call_target="tpu_custom_call", output_to_operand_aliasing={{}: (5, {})} | custom-call | flops 8589934592 | bytes 25165824 | tf_op jit(solution)/shard_map/gram/pallas_call | solution.py:293
  788.6 13.7 %all-to-all-done.5.refs_4_ = bf16[32,1,2,4,2,16,128]{6,5,4,3,2,1,0:T(8,128)(2,1)} async-done(((bf16[32,1,2,4,2,16,128]{6,5,4,3,2,1,0:T(8,128)(2,1)}), bf16[32,1,2,4,2,16,128]{6,5,4,3,2,1,0:T(8,128)(2,1)}, u32[]{:S(2)}, u32[]{:S(2)}) %all-to-all-start.5) | async-done | bytes 2097184 | tf_op jit(solution)/shard_map/all_to_all | solution.py:364
  802.3 11.7 %gram.7 = f32[32,2,512,512]{3,2,1,0:T(8,128)} custom-call(bf16[32,3,2,4,2,8,128]{6,5,4,3,2,1,0:T(8,128)(2,1)} %all-to-all-done.rest_0_.refs_5_.refs_0_, bf16[32,4,2,4,2,8,128]{6,5,4,3,2,1,0:T(8,128)(2,1)} %all-to-all-done.2.rest_1_.refs_5_.refs_6_.refs_1_, ...), custom_call_target="tpu_custom_call", output_to_operand_aliasing={{}: (5, {})} | custom-call | flops 8589934592 | bytes 25165824 | tf_op jit(solution)/shard_map/gram/pallas_call | solution.py:293
Async XLA Ops:
  22.9 33.7 %all-to-all-start.1 = ((bf16[32,1,2,4,2,8,128]{6,5,4,3,2,1,0:T(8,128)(2,1)}), bf16[32,1,2,4,2,8,128]{6,5,4,3,2,1,0:T(8,128)(2,1)}, u32[]{:S(2)}, u32[]{:S(2)}) async-start(bf16[32,1,2,4,2,8,128]{6,5,4,3,2,1,0:T(8,128)(2,1)} %dft.8), calls=%async_computation.1 | async-start | bytes 2097152 | tf_op jit(solution)/shard_map/all_to_all | solution.py:364
  56.6 75.2 %all-to-all-start = ((bf16[32,3,2,4,2,8,128]{6,5,4,3,2,1,0:T(8,128)(2,1)}), bf16[32,3,2,4,2,8,128]{6,5,4,3,2,1,0:T(8,128)(2,1)}, u32[]{:S(2)}, u32[]{:S(2)}) async-start(bf16[32,3,2,4,2,8,128]{6,5,4,3,2,1,0:T(8,128)(2,1)} %dft.7), calls=%async_computation | async-start | bytes 6291456 | tf_op jit(solution)/shard_map/all_to_all | solution.py:364
  131.8 97.9 %all-to-all-start.2 = ((bf16[32,4,2,4,2,8,128]{6,5,4,3,2,1,0:T(8,128)(2,1)}), bf16[32,4,2,4,2,8,128]{6,5,4,3,2,1,0:T(8,128)(2,1)}, u32[]{:S(2)}, u32[]{:S(2)}) async-start(bf16[32,4,2,4,2,8,128]{6,5,4,3,2,1,0:T(8,128)(2,1)} %dft.9), calls=%async_computation.2 | async-start | bytes 8388608 | tf_op jit(solution)/shard_map/all_to_all | solution.py:364
  229.7 190.1 %all-to-all-start.3 = ((bf16[32,4,2,4,2,16,128]{6,5,4,3,2,1,0:T(8,128)(2,1)}), bf16[32,4,2,4,2,16,128]{6,5,4,3,2,1,0:T(8,128)(2,1)}, u32[]{:S(2)}, u32[]{:S(2)}) async-start(bf16[32,4,2,4,2,16,128]{6,5,4,3,2,1,0:T(8,128)(2,1)} %dft.10), calls=%async_computation.3 | async-start | bytes 16777216 | tf_op jit(solution)/shard_map/all_to_all | solution.py:364
  233.8 9.3 %copy-start = (bf16[32,30720]{1,0:T(8,128)(2,1)S(1)}, bf16[32,30720]{1,0:T(8,128)(2,1)}, u32[]{:S(2)}) copy-start(bf16[32,30720]{1,0:T(8,128)(2,1)} %param.5) | copy-start | bytes 5898244
  236.9 6.2 collective-permute-start
  419.9 329.8 %all-to-all-start.4 = ((bf16[32,7,2,4,2,16,128]{6,5,4,3,2,1,0:T(8,128)(2,1)}), bf16[32,7,2,4,2,16,128]{6,5,4,3,2,1,0:T(8,128)(2,1)}, u32[]{:S(2)}, u32[]{:S(2)}) async-start(bf16[32,7,2,4,2,16,128]{6,5,4,3,2,1,0:T(8,128)(2,1)} %dft.12), calls=%async_computation.4 | async-start | bytes 29360128 | tf_op jit(solution)/shard_map/all_to_all | solution.py:364
  749.7 52.6 %all-to-all-start.5 = ((bf16[32,1,2,4,2,16,128]{6,5,4,3,2,1,0:T(8,128)(2,1)}), bf16[32,1,2,4,2,16,128]{6,5,4,3,2,1,0:T(8,128)(2,1)}, u32[]{:S(2)}, u32[]{:S(2)}) async-start(bf16[32,1,2,4,2,16,128]{6,5,4,3,2,1,0:T(8,128)(2,1)} %dft.13), calls=%async_computation.5 | async-start | bytes 4194304 | tf_op jit(solution)/shard_map/all_to_all | solution.py:364

commit v3 on v2

--- a/solution.py
+++ b/solution.py
@@ -1,4 +1,5 @@
 import functools
+import itertools
 import math
 
 import jax
@@ -15,12 +16,15 @@
 TAPS = 16
 FOLD = FFT_LEN // 2
 SPAN = 128
-GROUPS = 4
 BATCH = 8
 STRETCH = 32
 COLS = 256
 VMEM = 127 * 512 * 1024
 AXES = ("wide", "narrow")
+
+
+def group_count(n_dev):
+    return min(8, CHANNELS // n_dev // 2)
 
 
 def odd_stride(rows):
@@ -43,15 +47,17 @@
 
 def dft_table(n_dev):
     chan_dev = CHANNELS // n_dev
-    cg = chan_dev // GROUPS
+    n_groups = group_count(n_dev)
+    cg = chan_dev // n_groups
     g, p, d, h = np.meshgrid(
-        np.arange(GROUPS), np.arange(2), np.arange(n_dev), np.arange(cg // 2), indexing="ij"
+        np.arange(n_groups), np.arange(2), np.arange(n_dev), np.arange(cg // 2), indexing="ij"
     )
     chan = d * chan_dev + g * cg + 2 * h + p
     turns = chan[..., None] * np.arange(FOLD) % FFT_LEN
     angles = 2.0 * np.pi * turns / FFT_LEN
     table = np.stack([np.cos(angles), -np.sin(angles)], axis=-2) / math.sqrt(FFT_LEN)
-    return np.concatenate(split16(table.reshape(GROUPS, 2, CHANNELS // GROUPS, FOLD)), axis=2)
+    table = table.reshape(n_groups // 2, 2, 2, CHANNELS // n_groups, FOLD).swapaxes(1, 2)
+    return np.stack(split16(table), axis=2)
 
 
 def filter_kernel(first, n_in, with_after, x_ref, w_ref, halo_ref, *rest):
@@ -156,58 +162,66 @@
     folded, table_ref, (out_ref, held_ref) = refs[:4], refs[4], refs[-2:]
     step = pl.program_id(1)
     n_in = out_ref.shape[-2]
-    n_rows = table_ref.shape[2] // 2
+    n_groups, n_rows = table_ref.shape[3], table_ref.shape[3] * table_ref.shape[4]
     pitch = odd_stride(n_in)
     n_chunks, f_rows, _ = folded[0].shape
     n_here = f_rows // SPAN
 
     def product(p, low_too, chunk, ref, rows):
-        left = table_ref[0, p, : (1 + low_too) * n_rows, chunk * COLS : (chunk + 1) * COLS]
+        left = table_ref[0, p, : 1 + low_too, :, :, chunk * COLS : (chunk + 1) * COLS]
+        left = left.reshape(-1, COLS)
         dims = (((1,), (1,)), ((), ()))
         return lax.dot_general(left, ref[chunk, rows, :], dims, preferred_element_type=jnp.float32)
 
     for p in range(2):
+        high, low = folded[2 * p], folded[2 * p + 1]
         for pair in range(0, n_here, 2):
             take = min(2, n_here - pair)
             rows = pl.ds(pair * SPAN, take * SPAN)
-            both = sum(product(p, 1, chunk, folded[2 * p], rows) for chunk in range(n_chunks))
-            rest = sum(product(p, 0, chunk, folded[2 * p + 1], rows) for chunk in range(n_chunks))
+            both = sum(product(p, 1, chunk, high, rows) for chunk in range(n_chunks))
+            rest = sum(product(p, 0, chunk, low, rows) for chunk in range(n_chunks))
             total = both[:n_rows] + (both[n_rows:] + rest)
             for j in range(take):
-                at = step * n_here + pair + j
-                held_ref[p, pl.ds(at, n_rows, stride=pitch), :] = total[:, j * SPAN : (j + 1) * SPAN]
+                at = pl.ds(step * n_here + pair + j, n_rows, stride=pitch)
+                held_ref[p, at, :] = total[:, j * SPAN : (j + 1) * SPAN]
 
     @pl.when(step == pl.num_programs(1) - 1)
     def _():
         n_dev, _, _, n_pair, _, _, _ = out_ref.shape
-        for p in range(2):
-            for d in range(n_dev):
-                each = n_pair * 2 * pitch
-                block = held_ref[p, pl.ds(d * each, each), :].reshape(n_pair, 2, pitch, SPAN)
-                out_ref[d, 0, p] = block[:, :, :n_in].astype(jnp.bfloat16)
+        each = n_pair * 2 * pitch
+        for g, p, d in itertools.product(range(n_groups), range(2), range(n_dev)):
+            block = held_ref[p, pl.ds((g * n_dev + d) * each, each), :].reshape(n_pair, 2, pitch, SPAN)
+            out_ref[d, g, p] = block[:, :, :n_in].astype(jnp.bfloat16)
 
 
 def dft_unit(folded, table, n_dev, n_in, g0, n_groups, n_slots, slot, previous, deps):
     chan_dev = CHANNELS // n_dev
-    n_pair = chan_dev // GROUPS // 2
-    n_rows = CHANNELS // GROUPS
+    n_pair = chan_dev // group_count(n_dev) // 2
+    n_rows = CHANNELS // group_count(n_dev)
+    each = 1 if (g0 | n_groups | slot) % 2 else 2
     here = min(4, n_in)
     filled = [] if previous is None else [previous]
+
+    def table_at(g, i):
+        group = g0 + each * g
+        return (group // 2, 0, 0, group % 2 if each == 1 else 0, 0, 0)
+
     f_block = (FOLD // COLS, here * SPAN, COLS)
     return pl.pallas_call(
         dft_kernel,
-        grid=(n_groups, n_in // here),
+        grid=(n_groups // each, n_in // here),
         in_specs=[pl.BlockSpec(f_block, lambda g, i: (0, i, 0))] * 4
-        + [pl.BlockSpec((1, 2, 2 * n_rows, FOLD), lambda g, i: (g0 + g, 0, 0, 0))]
+        + [pl.BlockSpec((1, 2, 2, each, n_rows, FOLD), table_at)]
         + [pl.BlockSpec(memory_space=pl.ANY)] * (len(deps) + len(filled)),
         out_specs=pl.BlockSpec(
-            (n_dev, 1, 2, n_pair, 2, n_in, SPAN), lambda g, i: (0, slot + g, 0, 0, 0, 0, 0)
+            (n_dev, each, 2, n_pair, 2, n_in, SPAN),
+            lambda g, i: (0, slot // each + g, 0, 0, 0, 0, 0),
         ),
         out_shape=jax.ShapeDtypeStruct(
             (n_dev, n_slots, 2, n_pair, 2, n_in, SPAN), jnp.bfloat16
         ),
         input_output_aliases={5: 0} if filled else {},
-        scratch_shapes=[pltpu.VMEM((2, n_rows * odd_stride(n_in), SPAN), jnp.float32)],
+        scratch_shapes=[pltpu.VMEM((2, each * n_rows * odd_stride(n_in), SPAN), jnp.float32)],
         compiler_params=pltpu.CompilerParams(vmem_limit_bytes=VMEM),
         cost_estimate=pl.CostEstimate(
             flops=n_groups * 12 * n_rows * n_in * SPAN * FOLD,
@@ -275,7 +289,7 @@
 def gram_group(units, layout, places, previous, n_wide, n_narrow, halves, inputs, group):
     n_dev = n_wide * n_narrow
     chan_dev = CHANNELS // n_dev
-    cg = chan_dev // GROUPS
+    cg = chan_dev // group_count(n_dev)
     n_units = len(units)
     time_len = n_narrow * halves * SPAN
     specs = [
@@ -335,12 +349,16 @@
     ]
     if n_unit == 16:
         layout[:1] = [(0, 8, 0), (8, 8, 0)]
-    last = len(layout) - 1
-    parts = [[(0, 0, 1)], [(0, 1, GROUPS - 1)]]
-    parts += [[(index, 0, GROUPS)] for index in range(1, last - 1)]
-    parts += [[(last - 1, 0, GROUPS)]] if last > 1 else []
-    parts[-1:] = [parts[-1] + [(last, 0, GROUPS - 1)]] if last > 1 else [parts[-1], [(last, 0, GROUPS - 1)]]
-    parts += [[(last, GROUPS - 1, 1)]]
+    n_groups = group_count(n_dev)
+    head, last = n_groups // 4, len(layout) - 1
+    parts = [[(0, 0, head)], [(0, head, n_groups - head)]]
+    if last > 1:
+        parts += [[(index, 0, n_groups)] for index in range(1, last - 1)]
+        parts += [[(last - 1, 0, n_groups - 2), (last - 1, n_groups - 2, 1)]]
+        parts[-1] += [(last, n_groups - 2, 1), (last, 0, n_groups - 2)]
+        parts += [[(last - 1, n_groups - 1, 1), (last, n_groups - 1, 1)]]
+    else:
+        parts += [[(last, 0, n_groups - 1)], [(last, n_groups - 1, 1)]]
 
     received = []
     folded = {}
@@ -364,7 +382,7 @@
         received.append(lax.all_to_all(spectra, AXES, split_axis=0, concat_axis=0, tiled=True))
 
     result = None
-    for group in range(GROUPS):
+    for group in range(n_groups):
         found = [place[index, group] for index in range(len(layout))]
         units = [received[job] for job, _ in found]
         places = [slot for _, slot in found]

time: 815 us -> 811 us (level)
  waiting for transfers between devices: 449 us -> 416 us
  Pallas kernels: 331 us -> 360 us
    all_to_all x6, waiting for transfers between devices: 444 us -> 411 us  [shards(): lax.all_to_all(spectra, AXES, split_axis=0, concat_axis=0, tiled=True)]
    pallas_call x7 -> x10, Pallas kernels: 169 us -> 189 us  [dft_unit(): pl.pallas_call(dft_kernel, grid=(n_groups // each, n_in // here), in_spec...]
    pallas_call x4 -> x8, Pallas kernels: 46.9 us -> 57.2 us  [gram_group(): pl.pallas_call(functools.partial(gram_kernel, layout, halves, n_wide, n_n...]
  transfers between devices with their start and end apart: 7 -> 7, of which waited for: 7 -> 6; matrix products, arithmetic and copies ran while one was open for 1% -> 1% of each run, Pallas kernels for 36% -> 41%
where the time goes in v3:
time: 811 us
  waiting for transfers between devices  416 us (51%)
  Pallas kernels  360 us (44%)
  starting transfers between devices  28.3 us (3%)
    all_to_all x6, waiting for transfers between devices, shards(): lax.all_to_all(spectra, AXES, split_axis=0, concat_axis=0, tiled=True)  411 us
    pallas_call x10, Pallas kernels, dft_unit(): pl.pallas_call(dft_kernel, grid=(n_groups // each, n_in // here), in_spec...  189 us
    pallas_call x5, Pallas kernels, filter_unit(): pl.pallas_call(functools.partial(filter_kernel, start % n_block, n_in, wi...  115 us
    pallas_call x8, Pallas kernels, gram_group(): pl.pallas_call(functools.partial(gram_kernel, layout, halves, n_wide, n_n...  57.2 us
    all_to_all x6, starting transfers between devices, shards(): lax.all_to_all(spectra, AXES, split_axis=0, concat_axis=0, tiled=True)  26.9 us
  transfers between devices with their start and end apart: 7, of which 6 were waited for; matrix products, arithmetic and copies ran while one was open for 1% of the time, Pallas kernels for 41%

profile of v3, /device:TPU:0, one launch (start us, length us, event | category | flops | bytes accessed | tf_op | source)
XLA Modules:
  0.0 810.8 jit_solution(14380392908860544348)
XLA Ops:
  0.0 15.2 %filter.5 = (bf16[4,8,128,256]{3,2,1,0:T(8,128)(2,1)}, bf16[4,8,128,256]{3,2,1,0:T(8,128)(2,1)}, bf16[4,8,128,256]{3,2,1,0:T(8,128)(2,1)}, bf16[4,8,128,256]{3,2,1,0:T(8,128)(2,1)}) custom-call(bf16[32,524288]{1,0:T(8,128)(2,1)} %halo_ref.9, f32[16,8,2048]{2,1,0:T(8,128)} %constant.11.clone.w_ref, bf16[32,524288]{1,0:T(8,128)(2,1)} %halo_ref.9), custom_call_target="tpu_custom_call" | custom-call | flops 67108864 | bytes 12582912 | tf_op jit(solution)/shard_map/filter/pallas_call | solution.py:141
  15.2 7.7 dft.11
  22.9 7.4 all-to-all-start.1
  30.4 17.3 %dft.10 = bf16[32,6,2,2,2,8,128]{6,5,4,3,2,1,0:T(8,128)(2,1)} custom-call(bf16[4,1024,256]{2,1,0:T(8,128)(2,1)} %bitcast.45, bf16[4,1024,256]{2,1,0:T(8,128)(2,1)} %bitcast.47, bf16[4,1024,256]{2,1,0:T(8,128)(2,1)} %bitcast.49, bf16[4,1024,256]{2,1,0:T(8,128)(2,1)} %bitcast.51, bf16[4,2,2,2,128,1024]{5,4,3,2,1,0:T(8,128)(2,1)} %constant.10.clone.refs_4_), custom_call_target="tpu_custom_call" | custom-call | flops 9663676416 | bytes 50331648 | tf_op jit(solution)/shard_map/dft/pallas_call | solution.py:210
  47.6 9.0 %all-to-all-done.1.rest_0_.refs_5_.refs_0_ = bf16[32,2,2,2,2,8,128]{6,5,4,3,2,1,0:T(8,128)(2,1)} async-done(((bf16[32,2,2,2,2,8,128]{6,5,4,3,2,1,0:T(8,128)(2,1)}), bf16[32,2,2,2,2,8,128]{6,5,4,3,2,1,0:T(8,128)(2,1)}, u32[]{:S(2)}, u32[]{:S(2)}) %all-to-all-start.1) | async-done | bytes 1048608 | tf_op jit(solution)/shard_map/all_to_all | solution.py:382
  56.6 3.7 all-to-all-start
  60.3 15.3 %filter.6 = (bf16[4,8,128,256]{3,2,1,0:T(8,128)(2,1)}, bf16[4,8,128,256]{3,2,1,0:T(8,128)(2,1)}, bf16[4,8,128,256]{3,2,1,0:T(8,128)(2,1)}, bf16[4,8,128,256]{3,2,1,0:T(8,128)(2,1)}) custom-call(bf16[32,524288]{1,0:T(8,128)(2,1)} %halo_ref.9, f32[16,8,2048]{2,1,0:T(8,128)} %constant.11.clone.w_ref, bf16[32,524288]{1,0:T(8,128)(2,1)} %halo_ref.9, ...), custom_call_target="tpu_custom_call" | custom-call | flops 67108864 | bytes 12582912 | tf_op jit(solution)/shard_map/filter/pallas_call | solution.py:141
  75.6 22.0 %dft.12 = bf16[32,8,2,2,2,8,128]{6,5,4,3,2,1,0:T(8,128)(2,1)} custom-call(bf16[4,1024,256]{2,1,0:T(8,128)(2,1)} %bitcast.56, bf16[4,1024,256]{2,1,0:T(8,128)(2,1)} %bitcast.57, bf16[4,1024,256]{2,1,0:T(8,128)(2,1)} %bitcast.58, bf16[4,1024,256]{2,1,0:T(8,128)(2,1)} %bitcast.59, bf16[4,2,2,2,128,1024]{5,4,3,2,1,0:T(8,128)(2,1)} %constant.10.clone.refs_4_, ...), custom_call_target="tpu_custom_call" | custom-call | flops 12884901888 | bytes 67108864 | tf_op jit(solution)/shard_map/dft/pallas_call | solution.py:210
  97.6 34.2 %all-to-all-done.rest_0_.refs_5_.refs_0_ = bf16[32,6,2,2,2,8,128]{6,5,4,3,2,1,0:T(8,128)(2,1)} async-done(((bf16[32,6,2,2,2,8,128]{6,5,4,3,2,1,0:T(8,128)(2,1)}), bf16[32,6,2,2,2,8,128]{6,5,4,3,2,1,0:T(8,128)(2,1)}, u32[]{:S(2)}, u32[]{:S(2)}) %all-to-all-start) | async-done | bytes 3145760 | tf_op jit(solution)/shard_map/all_to_all | solution.py:382
  131.8 4.1 all-to-all-start.2
  135.9 27.7 %filter.7 = (bf16[4,16,128,256]{3,2,1,0:T(8,128)(2,1)}, bf16[4,16,128,256]{3,2,1,0:T(8,128)(2,1)}, bf16[4,16,128,256]{3,2,1,0:T(8,128)(2,1)}, bf16[4,16,128,256]{3,2,1,0:T(8,128)(2,1)}) custom-call(bf16[32,524288]{1,0:T(8,128)(2,1)} %halo_ref.9, f32[16,8,2048]{2,1,0:T(8,128)} %constant.11.clone.w_ref, bf16[32,524288]{1,0:T(8,128)(2,1)} %halo_ref.9, ...), custom_call_target="tpu_custom_call" | custom-call | flops 134217728 | bytes 25165824 | tf_op jit(solution)/shard_map/filter/pallas_call | solution.py:141
  163.6 39.8 %dft.13 = bf16[32,8,2,2,2,16,128]{6,5,4,3,2,1,0:T(8,128)(2,1)} custom-call(bf16[4,2048,256]{2,1,0:T(8,128)(2,1)} %bitcast.52, bf16[4,2048,256]{2,1,0:T(8,128)(2,1)} %bitcast.53, bf16[4,2048,256]{2,1,0:T(8,128)(2,1)} %bitcast.54, bf16[4,2048,256]{2,1,0:T(8,128)(2,1)} %bitcast.55, bf16[4,2,2,2,128,1024]{5,4,3,2,1,0:T(8,128)(2,1)} %constant.10.clone.refs_4_, ...), custom_call_target="tpu_custom_call" | custom-call | flops 25769803776 | bytes 134217728 | tf_op jit(solution)/shard_map/dft/pallas_call | solution.py:210
  203.4 26.3 %all-to-all-done.2.rest_1_.refs_5_.refs_6_.refs_1_ = bf16[32,8,2,2,2,8,128]{6,5,4,3,2,1,0:T(8,128)(2,1)} async-done(((bf16[32,8,2,2,2,8,128]{6,5,4,3,2,1,0:T(8,128)(2,1)}), bf16[32,8,2,2,2,8,128]{6,5,4,3,2,1,0:T(8,128)(2,1)}, u32[]{:S(2)}, u32[]{:S(2)}) %all-to-all-start.2) | async-done | bytes 4194336 | tf_op jit(solution)/shard_map/all_to_all | solution.py:382
  229.7 4.1 all-to-all-start.3
  233.8 0.0 copy-start
  233.8 3.1 slice.3
  236.9 1.5 collective-permute-start
  238.4 4.7 collective-permute-done
  243.1 0.0 copy-done
  243.1 3.0 broadcast_select_fusion.rest_0_
  246.1 28.2 %filter.9 = (bf16[4,16,128,256]{3,2,1,0:T(8,128)(2,1)}, bf16[4,16,128,256]{3,2,1,0:T(8,128)(2,1)}, bf16[4,16,128,256]{3,2,1,0:T(8,128)(2,1)}, bf16[4,16,128,256]{3,2,1,0:T(8,128)(2,1)}) custom-call(bf16[32,524288]{1,0:T(8,128)(2,1)} %halo_ref.9, f32[16,8,2048]{2,1,0:T(8,128)} %constant.11.clone.w_ref, bf16[32,524288]{1,0:T(8,128)(2,1)} %halo_ref.9, ...), custom_call_target="tpu_custom_call" | custom-call | flops 134217728 | bytes 25165824 | tf_op jit(solution)/shard_map/filter/pallas_call | solution.py:141
  274.4 28.2 %filter.8 = (bf16[4,16,128,256]{3,2,1,0:T(8,128)(2,1)}, bf16[4,16,128,256]{3,2,1,0:T(8,128)(2,1)}, bf16[4,16,128,256]{3,2,1,0:T(8,128)(2,1)}, bf16[4,16,128,256]{3,2,1,0:T(8,128)(2,1)}) custom-call(bf16[32,524288]{1,0:T(8,128)(2,1)} %halo_ref.9, f32[16,8,2048]{2,1,0:T(8,128)} %constant.11.clone.w_ref, bf16[32,524288]{1,0:T(8,128)(2,1)} %halo_ref.9, ...), custom_call_target="tpu_custom_call" | custom-call | flops 134217728 | bytes 25165824 | tf_op jit(solution)/shard_map/filter/pallas_call | solution.py:141
  302.6 30.7 %dft.16.refs_5_ = bf16[32,14,2,2,2,16,128]{6,5,4,3,2,1,0:T(8,128)(2,1)} custom-call(bf16[4,2048,256]{2,1,0:T(8,128)(2,1)} %bitcast.32, bf16[4,2048,256]{2,1,0:T(8,128)(2,1)} %bitcast.35, bf16[4,2048,256]{2,1,0:T(8,128)(2,1)} %bitcast.38, bf16[4,2048,256]{2,1,0:T(8,128)(2,1)} %bitcast.41, bf16[4,2,2,2,128,1024]{5,4,3,2,1,0:T(8,128)(2,1)} %constant.10.clone.refs_4_, ...), custom_call_target="tpu_custom_call" | custom-call | flops 19327352832 | bytes 100663296 | tf_op jit(solution)/shard_map/dft/pallas_call | solution.py:210
  333.3 10.1 %dft.17.refs_5_ = bf16[32,14,2,2,2,16,128]{6,5,4,3,2,1,0:T(8,128)(2,1)} custom-call(bf16[4,2048,256]{2,1,0:T(8,128)(2,1)} %bitcast.33, bf16[4,2048,256]{2,1,0:T(8,128)(2,1)} %bitcast.36, bf16[4,2048,256]{2,1,0:T(8,128)(2,1)} %bitcast.39, bf16[4,2048,256]{2,1,0:T(8,128)(2,1)} %bitcast.42, ...), custom_call_target="tpu_custom_call", output_to_operand_aliasing={{}: (5, {})} | custom-call | flops 3221225472 | bytes 16777216 | tf_op jit(solution)/shard_map/dft/pallas_call | solution.py:210
  343.3 10.1 %dft.18.refs_5_ = bf16[32,14,2,2,2,16,128]{6,5,4,3,2,1,0:T(8,128)(2,1)} custom-call(bf16[4,2048,256]{2,1,0:T(8,128)(2,1)} %bitcast.20, bf16[4,2048,256]{2,1,0:T(8,128)(2,1)} %bitcast.23, bf16[4,2048,256]{2,1,0:T(8,128)(2,1)} %bitcast.26, bf16[4,2048,256]{2,1,0:T(8,128)(2,1)} %bitcast.29, ...), custom_call_target="tpu_custom_call", output_to_operand_aliasing={{}: (5, {})} | custom-call | flops 3221225472 | bytes 16777216 | tf_op jit(solution)/shard_map/dft/pallas_call | solution.py:210
  353.4 30.6 %dft.19 = bf16[32,14,2,2,2,16,128]{6,5,4,3,2,1,0:T(8,128)(2,1)} custom-call(bf16[4,2048,256]{2,1,0:T(8,128)(2,1)} %bitcast.21, bf16[4,2048,256]{2,1,0:T(8,128)(2,1)} %bitcast.24, bf16[4,2048,256]{2,1,0:T(8,128)(2,1)} %bitcast.27, bf16[4,2048,256]{2,1,0:T(8,128)(2,1)} %bitcast.30, ...), custom_call_target="tpu_custom_call", output_to_operand_aliasing={{}: (5, {})} | custom-call | flops 19327352832 | bytes 100663296 | tf_op jit(solution)/shard_map/dft/pallas_call | solution.py:210
  384.1 35.8 %all-to-all-done.3.refs_5_.refs_6_.refs_2_ = bf16[32,8,2,2,2,16,128]{6,5,4,3,2,1,0:T(8,128)(2,1)} async-done(((bf16[32,8,2,2,2,16,128]{6,5,4,3,2,1,0:T(8,128)(2,1)}), bf16[32,8,2,2,2,16,128]{6,5,4,3,2,1,0:T(8,128)(2,1)}, u32[]{:S(2)}, u32[]{:S(2)}) %all-to-all-start.3) | async-done | bytes 8388640 | tf_op jit(solution)/shard_map/all_to_all | solution.py:382
  419.9 3.8 all-to-all-start.5
  423.7 10.1 %dft.14.refs_5_ = bf16[32,2,2,2,2,16,128]{6,5,4,3,2,1,0:T(8,128)(2,1)} custom-call(bf16[4,2048,256]{2,1,0:T(8,128)(2,1)} %bitcast.34, bf16[4,2048,256]{2,1,0:T(8,128)(2,1)} %bitcast.37, bf16[4,2048,256]{2,1,0:T(8,128)(2,1)} %bitcast.40, bf16[4,2048,256]{2,1,0:T(8,128)(2,1)} %bitcast.43, bf16[4,2,2,2,128,1024]{5,4,3,2,1,0:T(8,128)(2,1)} %constant.10.clone.refs_4_, ...), custom_call_target="tpu_custom_call" | custom-call | flops 3221225472 | bytes 16777216 | tf_op jit(solution)/shard_map/dft/pallas_call | solution.py:210
  433.8 10.2 %dft.15 = bf16[32,2,2,2,2,16,128]{6,5,4,3,2,1,0:T(8,128)(2,1)} custom-call(bf16[4,2048,256]{2,1,0:T(8,128)(2,1)} %bitcast.22, bf16[4,2048,256]{2,1,0:T(8,128)(2,1)} %bitcast.25, bf16[4,2048,256]{2,1,0:T(8,128)(2,1)} %bitcast.28, bf16[4,2048,256]{2,1,0:T(8,128)(2,1)} %bitcast.31, ...), custom_call_target="tpu_custom_call", output_to_operand_aliasing={{}: (5, {})} | custom-call | flops 3221225472 | bytes 16777216 | tf_op jit(solution)/shard_map/dft/pallas_call | solution.py:210
  444.0 305.7 %all-to-all-done.5.refs_3_.refs_4_ = bf16[32,14,2,2,2,16,128]{6,5,4,3,2,1,0:T(8,128)(2,1)} async-done(((bf16[32,14,2,2,2,16,128]{6,5,4,3,2,1,0:T(8,128)(2,1)}), bf16[32,14,2,2,2,16,128]{6,5,4,3,2,1,0:T(8,128)(2,1)}, u32[]{:S(2)}, u32[]{:S(2)}) %all-to-all-start.5) | async-done | bytes 14680096 | tf_op jit(solution)/shard_map/all_to_all | solution.py:382
  749.7 3.7 all-to-all-start.4
  753.4 7.1 gram.8.refs_5_
  760.5 7.1 gram.9.refs_5_
  767.6 7.1 gram.10.refs_5_
  774.8 7.1 gram.11.refs_5_
  781.9 7.1 gram.12.refs_5_
  789.0 7.1 gram.13.refs_5_
  796.1 7.4 gram.14.refs_5_
  803.5 0.0 all-to-all-done.4.refs_3_.refs_4_
  803.5 7.1 gram.15
Async XLA Ops:
  22.9 33.7 %all-to-all-start.1 = ((bf16[32,2,2,2,2,8,128]{6,5,4,3,2,1,0:T(8,128)(2,1)}), bf16[32,2,2,2,2,8,128]{6,5,4,3,2,1,0:T(8,128)(2,1)}, u32[]{:S(2)}, u32[]{:S(2)}) async-start(bf16[32,2,2,2,2,8,128]{6,5,4,3,2,1,0:T(8,128)(2,1)} %dft.11), calls=%async_computation.1 | async-start | bytes 2097152 | tf_op jit(solution)/shard_map/all_to_all | solution.py:382
  56.6 75.2 %all-to-all-start = ((bf16[32,6,2,2,2,8,128]{6,5,4,3,2,1,0:T(8,128)(2,1)}), bf16[32,6,2,2,2,8,128]{6,5,4,3,2,1,0:T(8,128)(2,1)}, u32[]{:S(2)}, u32[]{:S(2)}) async-start(bf16[32,6,2,2,2,8,128]{6,5,4,3,2,1,0:T(8,128)(2,1)} %dft.10), calls=%async_computation | async-start | bytes 6291456 | tf_op jit(solution)/shard_map/all_to_all | solution.py:382
  131.8 97.9 %all-to-all-start.2 = ((bf16[32,8,2,2,2,8,128]{6,5,4,3,2,1,0:T(8,128)(2,1)}), bf16[32,8,2,2,2,8,128]{6,5,4,3,2,1,0:T(8,128)(2,1)}, u32[]{:S(2)}, u32[]{:S(2)}) async-start(bf16[32,8,2,2,2,8,128]{6,5,4,3,2,1,0:T(8,128)(2,1)} %dft.12), calls=%async_computation.2 | async-start | bytes 8388608 | tf_op jit(solution)/shard_map/all_to_all | solution.py:382
  229.7 190.1 %all-to-all-start.3 = ((bf16[32,8,2,2,2,16,128]{6,5,4,3,2,1,0:T(8,128)(2,1)}), bf16[32,8,2,2,2,16,128]{6,5,4,3,2,1,0:T(8,128)(2,1)}, u32[]{:S(2)}, u32[]{:S(2)}) async-start(bf16[32,8,2,2,2,16,128]{6,5,4,3,2,1,0:T(8,128)(2,1)} %dft.13), calls=%async_computation.3 | async-start | bytes 16777216 | tf_op jit(solution)/shard_map/all_to_all | solution.py:382
  233.8 9.3 %copy-start = (bf16[32,30720]{1,0:T(8,128)(2,1)S(1)}, bf16[32,30720]{1,0:T(8,128)(2,1)}, u32[]{:S(2)}) copy-start(bf16[32,30720]{1,0:T(8,128)(2,1)} %param.5) | copy-start | bytes 5898244
  236.9 6.2 collective-permute-start
  419.9 329.8 %all-to-all-start.5 = ((bf16[32,14,2,2,2,16,128]{6,5,4,3,2,1,0:T(8,128)(2,1)}), bf16[32,14,2,2,2,16,128]{6,5,4,3,2,1,0:T(8,128)(2,1)}, u32[]{:S(2)}, u32[]{:S(2)}) async-start(bf16[32,14,2,2,2,16,128]{6,5,4,3,2,1,0:T(8,128)(2,1)} %dft.19), calls=%async_computation.5 | async-start | bytes 29360128 | tf_op jit(solution)/shard_map/all_to_all | solution.py:382
  749.7 53.8 %all-to-all-start.4 = ((bf16[32,2,2,2,2,16,128]{6,5,4,3,2,1,0:T(8,128)(2,1)}), bf16[32,2,2,2,2,16,128]{6,5,4,3,2,1,0:T(8,128)(2,1)}, u32[]{:S(2)}, u32[]{:S(2)}) async-start(bf16[32,2,2,2,2,16,128]{6,5,4,3,2,1,0:T(8,128)(2,1)} %dft.15), calls=%async_computation.4 | async-start | bytes 4194304 | tf_op jit(solution)/shard_map/all_to_all | solution.py:382

commit v4 on v3

--- a/solution.py
+++ b/solution.py
@@ -286,7 +286,7 @@
         wait_all(step)
 
 
-def gram_group(units, layout, places, previous, n_wide, n_narrow, halves, inputs, group):
+def gram_group(units, layout, places, previous, n_wide, n_narrow, halves, inputs, group, count):
     n_dev = n_wide * n_narrow
     chan_dev = CHANNELS // n_dev
     cg = chan_dev // group_count(n_dev)
@@ -294,7 +294,7 @@
     time_len = n_narrow * halves * SPAN
     specs = [
         pl.BlockSpec(
-            (n_dev, 1, 2, 1, 2, n_in, SPAN), lambda t, at=at: (0, at, 0, t, 0, 0, 0)
+            (n_dev, 1, 2, 1, 2, n_in, SPAN), lambda t, at=at: (0, at + t // (cg // 2), 0, t % (cg // 2), 0, 0, 0)
         )
         for at, (_, n_in, _) in zip(places, layout)
     ]
@@ -306,7 +306,7 @@
         aliases = {n_units: 0}
     return pl.pallas_call(
         functools.partial(gram_kernel, layout, halves, n_wide, n_narrow, time_len, group * cg),
-        grid=(cg // 2,),
+        grid=(count * (cg // 2),),
         in_specs=specs,
         out_specs=pl.BlockSpec(memory_space=pl.ANY),
         out_shape=jax.ShapeDtypeStruct((chan_dev, 2, inputs, inputs), jnp.float32),
@@ -318,8 +318,8 @@
         input_output_aliases=aliases,
         compiler_params=pltpu.CompilerParams(vmem_limit_bytes=VMEM),
         cost_estimate=pl.CostEstimate(
-            flops=cg * 8 * inputs * inputs * time_len,
-            bytes_accessed=cg * inputs * (8 * inputs + 4 * time_len),
+            flops=count * cg * 8 * inputs * inputs * time_len,
+            bytes_accessed=count * cg * inputs * (8 * inputs + 4 * time_len),
             transcendentals=0,
         ),
         name="gram",
@@ -350,8 +350,9 @@
     if n_unit == 16:
         layout[:1] = [(0, 8, 0), (8, 8, 0)]
     n_groups = group_count(n_dev)
-    head, last = n_groups // 4, len(layout) - 1
-    parts = [[(0, 0, head)], [(0, head, n_groups - head)]]
+    head, last = max(n_groups // 8, 1), len(layout) - 1
+    even = head + head % 2
+    parts = [[(0, 0, head)], [(0, even, n_groups - even), (0, head, even - head)]]
     if last > 1:
         parts += [[(index, 0, n_groups)] for index in range(1, last - 1)]
         parts += [[(last - 1, 0, n_groups - 2), (last - 1, n_groups - 2, 1)]]
@@ -382,12 +383,27 @@
         received.append(lax.all_to_all(spectra, AXES, split_axis=0, concat_axis=0, tiled=True))
 
     result = None
+    runs = []
     for group in range(n_groups):
         found = [place[index, group] for index in range(len(layout))]
+        if runs and found == [(job, slot + runs[-1][1]) for job, slot in runs[-1][2]]:
+            runs[-1][1] += 1
+        else:
+            runs.append([group, 1, found])
+    for group, count, found in runs:
         units = [received[job] for job, _ in found]
         places = [slot for _, slot in found]
         result = gram_group(
-            units, layout, places, result, n_wide, n_narrow, halves, n_wide * local_inputs, group
+            units,
+            layout,
+            places,
+            result,
+            n_wide,
+            n_narrow,
+            halves,
+            n_wide * local_inputs,
+            group,
+            count,
         )
     return result
 

time: 811 us -> 819 us (level)
    all_to_all x6, waiting for transfers between devices: 411 us -> 419 us  [shards(): lax.all_to_all(spectra, AXES, split_axis=0, concat_axis=0, tiled=True)]
    pallas_call x8 -> x5, Pallas kernels: 57.2 us -> 49.8 us  [gram_group(): pl.pallas_call(functools.partial(gram_kernel, layout, halves, n_wide, n_n...]
    pallas_call x10 -> x11, Pallas kernels: 189 us -> 193 us  [dft_unit(): pl.pallas_call(dft_kernel, grid=(n_groups // each, n_in // here), in_spec...]
  transfers between devices with their start and end apart: 7 -> 7, of which waited for: 6 -> 6; matrix products, arithmetic and copies ran while one was open for 1% -> 1% of each run, Pallas kernels for 41% -> 40%
where the time goes in v4:
time: 819 us
  waiting for transfers between devices  424 us (52%)
  Pallas kernels  358 us (44%)
  starting transfers between devices  30.5 us (4%)
    all_to_all x6, waiting for transfers between devices, shards(): lax.all_to_all(spectra, AXES, split_axis=0, concat_axis=0, tiled=True)  419 us
    pallas_call x11, Pallas kernels, dft_unit(): pl.pallas_call(dft_kernel, grid=(n_groups // each, n_in // here), in_spec...  193 us
    pallas_call x5, Pallas kernels, filter_unit(): pl.pallas_call(functools.partial(filter_kernel, start % n_block, n_in, wi...  115 us
    pallas_call x5, Pallas kernels, gram_group(): pl.pallas_call(functools.partial(gram_kernel, layout, halves, n_wide, n_n...  49.8 us
    all_to_all x6, starting transfers between devices, shards(): lax.all_to_all(spectra, AXES, split_axis=0, concat_axis=0, tiled=True)  29 us
  transfers between devices with their start and end apart: 7, of which 6 were waited for; matrix products, arithmetic and copies ran while one was open for 1% of the time, Pallas kernels for 40%

profile of v4, /device:TPU:0, one launch (start us, length us, event | category | flops | bytes accessed | tf_op | source)
XLA Modules:
  0.0 818.6 jit_solution(5868512428197570307)
XLA Ops:
  0.0 15.2 %filter.5 = (bf16[4,8,128,256]{3,2,1,0:T(8,128)(2,1)}, bf16[4,8,128,256]{3,2,1,0:T(8,128)(2,1)}, bf16[4,8,128,256]{3,2,1,0:T(8,128)(2,1)}, bf16[4,8,128,256]{3,2,1,0:T(8,128)(2,1)}) custom-call(bf16[32,524288]{1,0:T(8,128)(2,1)} %halo_ref.9, f32[16,8,2048]{2,1,0:T(8,128)} %constant.11.clone.w_ref, bf16[32,524288]{1,0:T(8,128)(2,1)} %halo_ref.9), custom_call_target="tpu_custom_call" | custom-call | flops 67108864 | bytes 12582912 | tf_op jit(solution)/shard_map/filter/pallas_call | solution.py:141
  15.2 6.1 dft.13
  21.4 7.4 all-to-all-start.1
  28.8 17.3 %dft.11.refs_5_ = bf16[32,7,2,2,2,8,128]{6,5,4,3,2,1,0:T(8,128)(2,1)} custom-call(bf16[4,1024,256]{2,1,0:T(8,128)(2,1)} %bitcast.45, bf16[4,1024,256]{2,1,0:T(8,128)(2,1)} %bitcast.48, bf16[4,1024,256]{2,1,0:T(8,128)(2,1)} %bitcast.51, bf16[4,1024,256]{2,1,0:T(8,128)(2,1)} %bitcast.54, bf16[4,2,2,2,128,1024]{5,4,3,2,1,0:T(8,128)(2,1)} %constant.10.clone.refs_4_), custom_call_target="tpu_custom_call" | custom-call | flops 9663676416 | bytes 50331648 | tf_op jit(solution)/shard_map/dft/pallas_call | solution.py:210
  46.0 6.2 dft.12
  52.2 0.0 all-to-all-done.1.rest_0_.refs_5_.refs_0_
  52.2 5.9 all-to-all-start
  58.1 15.3 %filter.6 = (bf16[4,8,128,256]{3,2,1,0:T(8,128)(2,1)}, bf16[4,8,128,256]{3,2,1,0:T(8,128)(2,1)}, bf16[4,8,128,256]{3,2,1,0:T(8,128)(2,1)}, bf16[4,8,128,256]{3,2,1,0:T(8,128)(2,1)}) custom-call(bf16[32,524288]{1,0:T(8,128)(2,1)} %halo_ref.9, f32[16,8,2048]{2,1,0:T(8,128)} %constant.11.clone.w_ref, bf16[32,524288]{1,0:T(8,128)(2,1)} %halo_ref.9, ...), custom_call_target="tpu_custom_call" | custom-call | flops 67108864 | bytes 12582912 | tf_op jit(solution)/shard_map/filter/pallas_call | solution.py:141
  73.3 22.0 %dft.14 = bf16[32,8,2,2,2,8,128]{6,5,4,3,2,1,0:T(8,128)(2,1)} custom-call(bf16[4,1024,256]{2,1,0:T(8,128)(2,1)} %bitcast.60, bf16[4,1024,256]{2,1,0:T(8,128)(2,1)} %bitcast.61, bf16[4,1024,256]{2,1,0:T(8,128)(2,1)} %bitcast.62, bf16[4,1024,256]{2,1,0:T(8,128)(2,1)} %bitcast.63, bf16[4,2,2,2,128,1024]{5,4,3,2,1,0:T(8,128)(2,1)} %constant.10.clone.refs_4_, ...), custom_call_target="tpu_custom_call" | custom-call | flops 12884901888 | bytes 67108864 | tf_op jit(solution)/shard_map/dft/pallas_call | solution.py:210
  95.3 45.4 %all-to-all-done.rest_0_.refs_5_.refs_0_ = bf16[32,7,2,2,2,8,128]{6,5,4,3,2,1,0:T(8,128)(2,1)} async-done(((bf16[32,7,2,2,2,8,128]{6,5,4,3,2,1,0:T(8,128)(2,1)}), bf16[32,7,2,2,2,8,128]{6,5,4,3,2,1,0:T(8,128)(2,1)}, u32[]{:S(2)}, u32[]{:S(2)}) %all-to-all-start) | async-done | bytes 3670048 | tf_op jit(solution)/shard_map/all_to_all | solution.py:383
  140.7 4.1 all-to-all-start.2
  144.8 27.7 %filter.7 = (bf16[4,16,128,256]{3,2,1,0:T(8,128)(2,1)}, bf16[4,16,128,256]{3,2,1,0:T(8,128)(2,1)}, bf16[4,16,128,256]{3,2,1,0:T(8,128)(2,1)}, bf16[4,16,128,256]{3,2,1,0:T(8,128)(2,1)}) custom-call(bf16[32,524288]{1,0:T(8,128)(2,1)} %halo_ref.9, f32[16,8,2048]{2,1,0:T(8,128)} %constant.11.clone.w_ref, bf16[32,524288]{1,0:T(8,128)(2,1)} %halo_ref.9, ...), custom_call_target="tpu_custom_call" | custom-call | flops 134217728 | bytes 25165824 | tf_op jit(solution)/shard_map/filter/pallas_call | solution.py:141
  172.6 39.8 %dft.15 = bf16[32,8,2,2,2,16,128]{6,5,4,3,2,1,0:T(8,128)(2,1)} custom-call(bf16[4,2048,256]{2,1,0:T(8,128)(2,1)} %bitcast.56, bf16[4,2048,256]{2,1,0:T(8,128)(2,1)} %bitcast.57, bf16[4,2048,256]{2,1,0:T(8,128)(2,1)} %bitcast.58, bf16[4,2048,256]{2,1,0:T(8,128)(2,1)} %bitcast.59, bf16[4,2,2,2,128,1024]{5,4,3,2,1,0:T(8,128)(2,1)} %constant.10.clone.refs_4_, ...), custom_call_target="tpu_custom_call" | custom-call | flops 25769803776 | bytes 134217728 | tf_op jit(solution)/shard_map/dft/pallas_call | solution.py:210
  212.4 26.3 %all-to-all-done.2.rest_1_.refs_5_.refs_6_.refs_1_ = bf16[32,8,2,2,2,8,128]{6,5,4,3,2,1,0:T(8,128)(2,1)} async-done(((bf16[32,8,2,2,2,8,128]{6,5,4,3,2,1,0:T(8,128)(2,1)}), bf16[32,8,2,2,2,8,128]{6,5,4,3,2,1,0:T(8,128)(2,1)}, u32[]{:S(2)}, u32[]{:S(2)}) %all-to-all-start.2) | async-done | bytes 4194336 | tf_op jit(solution)/shard_map/all_to_all | solution.py:383
  238.7 4.1 all-to-all-start.3
  242.8 0.0 copy-start
  242.8 3.1 slice.3
  245.9 1.5 collective-permute-start
  247.4 4.7 collective-permute-done
  252.1 0.0 copy-done
  252.1 3.0 broadcast_select_fusion.rest_0_
  255.1 28.2 %filter.9 = (bf16[4,16,128,256]{3,2,1,0:T(8,128)(2,1)}, bf16[4,16,128,256]{3,2,1,0:T(8,128)(2,1)}, bf16[4,16,128,256]{3,2,1,0:T(8,128)(2,1)}, bf16[4,16,128,256]{3,2,1,0:T(8,128)(2,1)}) custom-call(bf16[32,524288]{1,0:T(8,128)(2,1)} %halo_ref.9, f32[16,8,2048]{2,1,0:T(8,128)} %constant.11.clone.w_ref, bf16[32,524288]{1,0:T(8,128)(2,1)} %halo_ref.9, ...), custom_call_target="tpu_custom_call" | custom-call | flops 134217728 | bytes 25165824 | tf_op jit(solution)/shard_map/filter/pallas_call | solution.py:141
  283.4 28.2 %filter.8 = (bf16[4,16,128,256]{3,2,1,0:T(8,128)(2,1)}, bf16[4,16,128,256]{3,2,1,0:T(8,128)(2,1)}, bf16[4,16,128,256]{3,2,1,0:T(8,128)(2,1)}, bf16[4,16,128,256]{3,2,1,0:T(8,128)(2,1)}) custom-call(bf16[32,524288]{1,0:T(8,128)(2,1)} %halo_ref.9, f32[16,8,2048]{2,1,0:T(8,128)} %constant.11.clone.w_ref, bf16[32,524288]{1,0:T(8,128)(2,1)} %halo_ref.9, ...), custom_call_target="tpu_custom_call" | custom-call | flops 134217728 | bytes 25165824 | tf_op jit(solution)/shard_map/filter/pallas_call | solution.py:141
  311.6 30.7 %dft.18.refs_5_ = bf16[32,14,2,2,2,16,128]{6,5,4,3,2,1,0:T(8,128)(2,1)} custom-call(bf16[4,2048,256]{2,1,0:T(8,128)(2,1)} %bitcast.32, bf16[4,2048,256]{2,1,0:T(8,128)(2,1)} %bitcast.35, bf16[4,2048,256]{2,1,0:T(8,128)(2,1)} %bitcast.38, bf16[4,2048,256]{2,1,0:T(8,128)(2,1)} %bitcast.41, bf16[4,2,2,2,128,1024]{5,4,3,2,1,0:T(8,128)(2,1)} %constant.10.clone.refs_4_, ...), custom_call_target="tpu_custom_call" | custom-call | flops 19327352832 | bytes 100663296 | tf_op jit(solution)/shard_map/dft/pallas_call | solution.py:210
  342.2 10.1 %dft.19.refs_5_ = bf16[32,14,2,2,2,16,128]{6,5,4,3,2,1,0:T(8,128)(2,1)} custom-call(bf16[4,2048,256]{2,1,0:T(8,128)(2,1)} %bitcast.33, bf16[4,2048,256]{2,1,0:T(8,128)(2,1)} %bitcast.36, bf16[4,2048,256]{2,1,0:T(8,128)(2,1)} %bitcast.39, bf16[4,2048,256]{2,1,0:T(8,128)(2,1)} %bitcast.42, ...), custom_call_target="tpu_custom_call", output_to_operand_aliasing={{}: (5, {})} | custom-call | flops 3221225472 | bytes 16777216 | tf_op jit(solution)/shard_map/dft/pallas_call | solution.py:210
  352.3 10.1 %dft.20.refs_5_ = bf16[32,14,2,2,2,16,128]{6,5,4,3,2,1,0:T(8,128)(2,1)} custom-call(bf16[4,2048,256]{2,1,0:T(8,128)(2,1)} %bitcast.20, bf16[4,2048,256]{2,1,0:T(8,128)(2,1)} %bitcast.23, bf16[4,2048,256]{2,1,0:T(8,128)(2,1)} %bitcast.26, bf16[4,2048,256]{2,1,0:T(8,128)(2,1)} %bitcast.29, ...), custom_call_target="tpu_custom_call", output_to_operand_aliasing={{}: (5, {})} | custom-call | flops 3221225472 | bytes 16777216 | tf_op jit(solution)/shard_map/dft/pallas_call | solution.py:210
  362.4 30.6 %dft.21 = bf16[32,14,2,2,2,16,128]{6,5,4,3,2,1,0:T(8,128)(2,1)} custom-call(bf16[4,2048,256]{2,1,0:T(8,128)(2,1)} %bitcast.21, bf16[4,2048,256]{2,1,0:T(8,128)(2,1)} %bitcast.24, bf16[4,2048,256]{2,1,0:T(8,128)(2,1)} %bitcast.27, bf16[4,2048,256]{2,1,0:T(8,128)(2,1)} %bitcast.30, ...), custom_call_target="tpu_custom_call", output_to_operand_aliasing={{}: (5, {})} | custom-call | flops 19327352832 | bytes 100663296 | tf_op jit(solution)/shard_map/dft/pallas_call | solution.py:210
  393.1 35.8 %all-to-all-done.3.refs_5_.refs_6_.refs_2_ = bf16[32,8,2,2,2,16,128]{6,5,4,3,2,1,0:T(8,128)(2,1)} async-done(((bf16[32,8,2,2,2,16,128]{6,5,4,3,2,1,0:T(8,128)(2,1)}), bf16[32,8,2,2,2,16,128]{6,5,4,3,2,1,0:T(8,128)(2,1)}, u32[]{:S(2)}, u32[]{:S(2)}) %all-to-all-start.3) | async-done | bytes 8388640 | tf_op jit(solution)/shard_map/all_to_all | solution.py:383
  428.9 3.8 all-to-all-start.5
  432.7 10.2 %dft.16.refs_5_ = bf16[32,2,2,2,2,16,128]{6,5,4,3,2,1,0:T(8,128)(2,1)} custom-call(bf16[4,2048,256]{2,1,0:T(8,128)(2,1)} %bitcast.34, bf16[4,2048,256]{2,1,0:T(8,128)(2,1)} %bitcast.37, bf16[4,2048,256]{2,1,0:T(8,128)(2,1)} %bitcast.40, bf16[4,2048,256]{2,1,0:T(8,128)(2,1)} %bitcast.43, bf16[4,2,2,2,128,1024]{5,4,3,2,1,0:T(8,128)(2,1)} %constant.10.clone.refs_4_, ...), custom_call_target="tpu_custom_call" | custom-call | flops 3221225472 | bytes 16777216 | tf_op jit(solution)/shard_map/dft/pallas_call | solution.py:210
  442.9 10.1 %dft.17 = bf16[32,2,2,2,2,16,128]{6,5,4,3,2,1,0:T(8,128)(2,1)} custom-call(bf16[4,2048,256]{2,1,0:T(8,128)(2,1)} %bitcast.22, bf16[4,2048,256]{2,1,0:T(8,128)(2,1)} %bitcast.25, bf16[4,2048,256]{2,1,0:T(8,128)(2,1)} %bitcast.28, bf16[4,2048,256]{2,1,0:T(8,128)(2,1)} %bitcast.31, ...), custom_call_target="tpu_custom_call", output_to_operand_aliasing={{}: (5, {})} | custom-call | flops 3221225472 | bytes 16777216 | tf_op jit(solution)/shard_map/dft/pallas_call | solution.py:210
  453.0 305.7 %all-to-all-done.5.refs_3_.refs_4_ = bf16[32,14,2,2,2,16,128]{6,5,4,3,2,1,0:T(8,128)(2,1)} async-done(((bf16[32,14,2,2,2,16,128]{6,5,4,3,2,1,0:T(8,128)(2,1)}), bf16[32,14,2,2,2,16,128]{6,5,4,3,2,1,0:T(8,128)(2,1)}, u32[]{:S(2)}, u32[]{:S(2)}) %all-to-all-start.5) | async-done | bytes 14680096 | tf_op jit(solution)/shard_map/all_to_all | solution.py:383
  758.7 3.7 all-to-all-start.4
  762.4 7.2 gram.5.refs_5_
  769.5 7.2 gram.6.refs_5_
  776.7 21.2 %gram.7.refs_5_ = f32[32,2,512,512]{3,2,1,0:T(8,128)} custom-call(bf16[32,7,2,2,2,8,128]{6,5,4,3,2,1,0:T(8,128)(2,1)} %all-to-all-done.rest_0_.refs_5_.refs_0_, bf16[32,8,2,2,2,8,128]{6,5,4,3,2,1,0:T(8,128)(2,1)} %all-to-all-done.2.rest_1_.refs_5_.refs_6_.refs_1_, ...), custom_call_target="tpu_custom_call", output_to_operand_aliasing={{}: (5, {})} | custom-call | flops 17179869184 | bytes 50331648 | tf_op jit(solution)/shard_map/gram/pallas_call | solution.py:307
  797.9 7.2 gram.8.refs_5_
  805.1 6.2 all-to-all-done.4.refs_3_.refs_4_
  811.3 7.1 gram.9
Async XLA Ops:
  21.4 30.9 %all-to-all-start.1 = ((bf16[32,1,2,2,2,8,128]{6,5,4,3,2,1,0:T(8,128)(2,1)}), bf16[32,1,2,2,2,8,128]{6,5,4,3,2,1,0:T(8,128)(2,1)}, u32[]{:S(2)}, u32[]{:S(2)}) async-start(bf16[32,1,2,2,2,8,128]{6,5,4,3,2,1,0:T(8,128)(2,1)} %dft.13), calls=%async_computation.1 | async-start | bytes 1048576 | tf_op jit(solution)/shard_map/all_to_all | solution.py:383
  52.2 88.5 %all-to-all-start = ((bf16[32,7,2,2,2,8,128]{6,5,4,3,2,1,0:T(8,128)(2,1)}), bf16[32,7,2,2,2,8,128]{6,5,4,3,2,1,0:T(8,128)(2,1)}, u32[]{:S(2)}, u32[]{:S(2)}) async-start(bf16[32,7,2,2,2,8,128]{6,5,4,3,2,1,0:T(8,128)(2,1)} %dft.12), calls=%async_computation | async-start | bytes 7340032 | tf_op jit(solution)/shard_map/all_to_all | solution.py:383
  140.7 98.0 %all-to-all-start.2 = ((bf16[32,8,2,2,2,8,128]{6,5,4,3,2,1,0:T(8,128)(2,1)}), bf16[32,8,2,2,2,8,128]{6,5,4,3,2,1,0:T(8,128)(2,1)}, u32[]{:S(2)}, u32[]{:S(2)}) async-start(bf16[32,8,2,2,2,8,128]{6,5,4,3,2,1,0:T(8,128)(2,1)} %dft.14), calls=%async_computation.2 | async-start | bytes 8388608 | tf_op jit(solution)/shard_map/all_to_all | solution.py:383
  238.7 190.1 %all-to-all-start.3 = ((bf16[32,8,2,2,2,16,128]{6,5,4,3,2,1,0:T(8,128)(2,1)}), bf16[32,8,2,2,2,16,128]{6,5,4,3,2,1,0:T(8,128)(2,1)}, u32[]{:S(2)}, u32[]{:S(2)}) async-start(bf16[32,8,2,2,2,16,128]{6,5,4,3,2,1,0:T(8,128)(2,1)} %dft.15), calls=%async_computation.3 | async-start | bytes 16777216 | tf_op jit(solution)/shard_map/all_to_all | solution.py:383
  242.8 9.3 %copy-start = (bf16[32,30720]{1,0:T(8,128)(2,1)S(1)}, bf16[32,30720]{1,0:T(8,128)(2,1)}, u32[]{:S(2)}) copy-start(bf16[32,30720]{1,0:T(8,128)(2,1)} %param.5) | copy-start | bytes 5898244
  245.9 6.2 collective-permute-start
  428.9 329.8 %all-to-all-start.5 = ((bf16[32,14,2,2,2,16,128]{6,5,4,3,2,1,0:T(8,128)(2,1)}), bf16[32,14,2,2,2,16,128]{6,5,4,3,2,1,0:T(8,128)(2,1)}, u32[]{:S(2)}, u32[]{:S(2)}) async-start(bf16[32,14,2,2,2,16,128]{6,5,4,3,2,1,0:T(8,128)(2,1)} %dft.21), calls=%async_computation.5 | async-start | bytes 29360128 | tf_op jit(solution)/shard_map/all_to_all | solution.py:383
  758.7 52.6 %all-to-all-start.4 = ((bf16[32,2,2,2,2,16,128]{6,5,4,3,2,1,0:T(8,128)(2,1)}), bf16[32,2,2,2,2,16,128]{6,5,4,3,2,1,0:T(8,128)(2,1)}, u32[]{:S(2)}, u32[]{:S(2)}) async-start(bf16[32,2,2,2,2,16,128]{6,5,4,3,2,1,0:T(8,128)(2,1)} %dft.17), calls=%async_computation.4 | async-start | bytes 4194304 | tf_op jit(solution)/shard_map/all_to_all | solution.py:383
